TPU v7x, 128 devices: a whole 4x4x4 slice. The times are simulated.
128 devices in a mesh: dp: 2 (over core), pipe: 4 (over z), expert: 16 (over y, x).
Axes of the slice: x: 4, y: 4, z: 4, core: 2. Of those that a mesh axis runs over, the one named last changes fastest.
Arguments:
- out_grad: bfloat16 [4, 4096, 2560], P('pipe', ('dp', 'expert')), may hold values from -6 to 6
- routes: int32 [4, 4096, 6], P('pipe', ('dp', 'expert')), may hold values from 0 to 15, all different within a row; in each aligned block of 128 rows (0 to 127, 128 to 255, ..., all dimensions but the last counted through in order) at most 64 rows name the same one
- combine: bfloat16 [4, 4096, 6], P('pipe', ('dp', 'expert')), may hold values from 0.049804688 to 0.5
- gate_up_weight: bfloat16 [4, 16, 2560, 1792], P('pipe', 'expert', 'dp'), may hold values from -0.125 to 0.125
- down_weight: bfloat16 [4, 16, 896, 2560], P('pipe', 'expert', None, 'dp'), may hold values from -0.1875 to 0.1875
- saved_inputs: bfloat16 [4, 2, 16, 1024, 2560], P('pipe', 'dp', 'expert'), may hold values from -6 to 6
- saved_gate_up: bfloat16 [4, 2, 16, 1024, 1792], P('pipe', 'dp', 'expert'), may hold values from -6 to 6
Outputs:
- passed_grad: bfloat16 [4, 4096, 2560], P('pipe', ('dp', 'expert'))
- combine_grad: bfloat16 [4, 4096, 6], P('pipe', ('dp', 'expert'))
- gate_up_grad: bfloat16 [4, 16, 2560, 1792], P('pipe', 'expert', 'dp')
- down_grad: bfloat16 [4, 16, 896, 2560], P('pipe', 'expert', None, 'dp')
Inputs may be any that keep to these rules, and one draw needn't show every extreme that they name: `routes`: the 6 numbers of a row differ. In each aligned block of 128 rows of a section no expert is named by more than 64 rows, and some block of every draw names some expert exactly 64 times.
All inputs are finite; a program needn't handle non-finite values.
Results may differ from a plain program's by a relative error of at most 0.0059.
Values may be sent and summed in bfloat16 or wider, within the bound.
A program may use at most 192 MiB of HBM per device.

v0:
```python
import jax
import jax.numpy as jnp
from jax import lax
from jax.sharding import PartitionSpec as P

SLOT = 64


def shifted(block, axis, distance):
    devices = range(lax.axis_size(axis))
    route = [((i - distance) % len(devices), i) for i in devices]
    return lax.ppermute(block, axis, route)


def slot_numbers(route_flat, experts):
    onehot = (route_flat[:, None] == jnp.arange(experts, dtype=jnp.int32)[None, :]).astype(
        jnp.int32
    )
    running = jnp.cumsum(onehot, axis=0)
    return jnp.sum(running * onehot, axis=1) - 1


def rounded(values):
    return lax.optimization_barrier(values.astype(jnp.bfloat16)).astype(jnp.float32)


def expert_rows(gu_rows, grad_rows, weight_rows, gate_up, down_proj):
    hidden_width = down_proj.shape[0]
    gate_pre = gu_rows[:, :hidden_width].astype(jnp.float32)
    up_pre = gu_rows[:, hidden_width:].astype(jnp.float32)
    logistic = jax.nn.sigmoid(gate_pre)
    activated = gate_pre * logistic
    hidden = activated * up_pre
    through = lax.dot_general(
        grad_rows, down_proj, (((1,), (1,)), ((), ())), preferred_element_type=jnp.float32
    )
    comb_part = jnp.sum(through * hidden, axis=1).astype(jnp.bfloat16)
    factor = weight_rows.astype(jnp.float32)[:, None]
    scaled = (factor * hidden).astype(jnp.bfloat16)
    grad_hidden = factor * through
    grad_gate = grad_hidden * up_pre * logistic * (1.0 + gate_pre * (1.0 - logistic))
    grad_up = grad_hidden * activated
    grad_gu = jnp.concatenate([grad_gate, grad_up], axis=1).astype(jnp.bfloat16)
    input_grad = lax.dot_general(
        grad_gu, gate_up, (((1,), (1,)), ((), ())), preferred_element_type=jnp.float32
    ).astype(jnp.bfloat16)
    return (input_grad, comb_part, grad_gu, scaled)


def body(out_grad, routes, combine, gate_up_weight, down_weight, saved_inputs, saved_gate_up):
    sources = lax.axis_size("expert")
    tok_rows = out_grad.shape[1]
    model_width = out_grad.shape[2]
    top_count = routes.shape[2]
    per_device = gate_up_weight.shape[1]
    experts = per_device * sources
    slot_cap = SLOT
    row_count = sources * slot_cap
    buffer_rows = experts * slot_cap
    gate_up, down_proj = (
        lax.all_gather(gate_up_weight[0], "dp", axis=1, tiled=True),
        lax.all_gather(down_weight[0], "dp", axis=2, tiled=True),
    )
    route_flat = routes[0].reshape(-1)
    slot_ids = slot_numbers(route_flat, experts)
    within = route_flat % per_device
    target = route_flat // per_device
    row_of = ((within * sources + target) * slot_cap + slot_ids).reshape(tok_rows, top_count)
    buffer_ids = jnp.arange(buffer_rows, dtype=jnp.int32)
    matches = [
        (buffer_ids[:, None] == row_of[None, :, pick]).astype(jnp.bfloat16)
        for pick in range(top_count)
    ]
    token_map = matches[0]
    for pick in range(1, top_count):
        token_map = token_map + matches[pick]
    grad_tok = out_grad[0]
    comb_tok = combine[0]
    send_grad = jnp.dot(token_map, grad_tok, preferred_element_type=jnp.float32).astype(
        jnp.bfloat16
    )
    send_weight = jnp.dot(matches[0], comb_tok[:, 0], preferred_element_type=jnp.float32)
    for pick in range(1, top_count):
        send_weight = send_weight + jnp.dot(
            matches[pick], comb_tok[:, pick], preferred_element_type=jnp.float32
        )
    send_grad = send_grad.reshape(per_device, sources, slot_cap, model_width)
    send_weight = send_weight.astype(jnp.bfloat16).reshape(per_device, sources, slot_cap)
    recv_grad, recv_weight = (
        lax.all_to_all(send_grad, "expert", split_axis=1, concat_axis=1, tiled=True),
        lax.all_to_all(send_weight, "expert", split_axis=1, concat_axis=1, tiled=True),
    )
    expert_dy = recv_grad.reshape(per_device, row_count, model_width)
    expert_w = recv_weight.reshape(per_device, row_count)
    expert_in = saved_inputs[0, 0]
    expert_gu = saved_gate_up[0, 0]
    outcome = expert_rows(expert_gu[0], expert_dy[0], expert_w[0], gate_up[0], down_proj[0])
    results = [outcome]
    input_grad = jnp.stack([outcome[0] for outcome in results])
    comb_part = jnp.stack([outcome[1] for outcome in results])
    grad_gu = jnp.stack([outcome[2] for outcome in results])
    scaled = jnp.stack([outcome[3] for outcome in results])
    back_grad, back_comb = (
        lax.all_to_all(
            input_grad.reshape(per_device, sources, slot_cap, model_width),
            "expert",
            split_axis=1,
            concat_axis=1,
            tiled=True,
        ),
        lax.all_to_all(
            comb_part.reshape(per_device, sources, slot_cap),
            "expert",
            split_axis=1,
            concat_axis=1,
            tiled=True,
        ),
    )
    back_flat = back_grad.reshape(buffer_rows, model_width)
    comb_flat = back_comb.reshape(buffer_rows)
    layer_grad = lax.dot_general(
        token_map, back_flat, (((0,), (0,)), ((), ())), preferred_element_type=jnp.float32
    ).astype(jnp.bfloat16)
    passed = shifted(layer_grad[None], "pipe", -1)
    comb_cols = [
        lax.dot_general(
            matches[pick], comb_flat, (((0,), (0,)), ((), ())), preferred_element_type=jnp.float32
        )
        for pick in range(top_count)
    ]
    comb_grad = jnp.stack(comb_cols, axis=1).astype(jnp.bfloat16).reshape(1, tok_rows, top_count)
    part_gu = rounded(
        jnp.einsum("erd,erf->edf", expert_in, grad_gu, preferred_element_type=jnp.float32)
    )
    part_down = rounded(
        jnp.einsum("erf,erd->efd", scaled, expert_dy, preferred_element_type=jnp.float32)
    )
    sum_gu, sum_down = (
        lax.psum_scatter(
            part_gu.astype(jnp.bfloat16), "dp", scatter_dimension=1, tiled=True
        ).astype(jnp.float32),
        lax.psum_scatter(
            part_down.astype(jnp.bfloat16), "dp", scatter_dimension=2, tiled=True
        ).astype(jnp.float32),
    )
    return (
        passed,
        comb_grad,
        sum_gu.astype(jnp.bfloat16)[None],
        sum_down.astype(jnp.bfloat16)[None],
    )


def solution(mesh):
    placed = (
        P("pipe", ("dp", "expert"), None),
        P("pipe", ("dp", "expert"), None),
        P("pipe", ("dp", "expert"), None),
        P("pipe", "expert", "dp", None),
        P("pipe", "expert", None, "dp"),
        P("pipe", "dp", "expert", None, None),
        P("pipe", "dp", "expert", None, None),
    )
    return jax.shard_map(
        body,
        mesh=mesh,
        in_specs=placed,
        out_specs=(
            P("pipe", ("dp", "expert"), None),
            P("pipe", ("dp", "expert"), None),
            P("pipe", "expert", "dp", None),
            P("pipe", "expert", None, "dp"),
        ),
        check_vma=False,
    )
```

profile of v0, /device:TPU:0, one launch (start us, length us, event | category | flops | bytes accessed | tf_op | source)
XLA Modules:
  0.0 283.8 jit_solution(11357535635285881501)
XLA Ops:
  7.2 0.0 copy-start
  7.2 0.0 copy-start.2
  7.2 0.0 copy-start.3
  7.2 0.0 all-gather.5.cloned.1.call-start
  7.2 0.7 all-gather.5.cloned.1.call-update
  7.9 0.0 all-gather.7.cloned.1.call-start
  8.0 0.7 all-gather.7.cloned.1.call-update
  8.7 0.0 copy-done.2
  8.7 0.1 copy.33
  8.8 0.1 eq.118
  8.9 0.1 eq.122
  9.1 1.7 reduce-window.6
  10.8 0.3 slice_reduce_fusion.6
  11.1 0.1 fusion.65
  11.2 0.1 sub.14
  11.4 0.3 slice_reduce_fusion.5
  11.7 0.0 copy-done.3
  11.7 0.2 fusion.33
  11.9 0.2 fusion.35
  12.1 0.2 fusion.37
  12.3 0.2 fusion.39
  12.5 0.2 fusion.43
  12.8 0.2 fusion.41
  13.0 0.7 reshape.217
  13.7 7.1 %all-to-all-start = ((bf16[1,16,64]{2,0,1:T(2,128)(2,1)}), bf16[1,16,64]{2,0,1:T(2,128)(2,1)S(1)}, u32[]{:S(2)}, u32[]{:S(2)}) async-start(bf16[1,16,64]{2,0,1:T(2,128)(2,1)} %reshape.217), calls=%async_computation | async-start | bytes 16384 | tf_op jit(solution)/shard_map/all_to_all | solution.py:91
  20.8 0.0 copy-done
  20.8 4.2 %convolution_convert_fusion.1 = bf16[1024,2560]{1,0:T(8,128)(2,1)} fusion(bf16[1,128,2560]{2,1,0:T(8,128)(2,1)S(1)} %copy-done, s32[128]{0:T(128)S(1)} %get-tuple-element.25, s32[128]{0:T(128)S(1)} %get-tuple-element.26, s32[128]{0:T(128)S(1)} %get-tuple-element.27, s32[128]{0:T(128)S(1)} %get-tuple-element.28, s32[128]{0:T(128)S(1)} %get-tuple-element.29, ...), kind=kOutput, calls=%fused_computation.4 | convolution fusion | flops 676855808 | bytes 5901312 | tf_op jit(solution)/shard_map/dot_general | solution.py:79
  25.0 3.3 %all-to-all-done = bf16[1,16,64]{2,0,1:T(2,128)(2,1)S(1)} async-done(((bf16[1,16,64]{2,0,1:T(2,128)(2,1)}), bf16[1,16,64]{2,0,1:T(2,128)(2,1)S(1)}, u32[]{:S(2)}, u32[]{:S(2)}) %all-to-all-start) | async-done | bytes 2080 | tf_op jit(solution)/shard_map/all_to_all | solution.py:91
  28.3 4.6 %all-to-all-start.1 = ((bf16[1,16,64,2560]{3,2,0,1:T(8,128)(2,1)}), bf16[1,16,64,2560]{3,2,0,1:T(8,128)(2,1)}, u32[]{:S(2)}, u32[]{:S(2)}) async-start(bf16[1,16,64,2560]{3,2,0,1:T(8,128)(2,1)} %bitcast.123), calls=%async_computation.1 | async-start | bytes 10485760 | tf_op jit(solution)/shard_map/all_to_all | solution.py:90
  32.9 0.2 reduce-scatter.3.cloned.1.call-start
  33.1 5.9 %copy.39 = bf16[1,1,1,1024,1792]{3,4,2,1,0:T(8,128)(2,1)} copy(bf16[1,1,1,1024,1792]{4,3,2,1,0:T(8,128)(2,1)} %param.13) | data formatting | bytes 7340032 | tf_op args[6]
  39.1 0.1 reshape.188
  39.1 0.0 all-gather.5.cloned.1.call-done
  39.1 69.6 %all-to-all-done.1 = bf16[1,16,64,2560]{3,2,0,1:T(8,128)(2,1)} async-done(((bf16[1,16,64,2560]{3,2,0,1:T(8,128)(2,1)}), bf16[1,16,64,2560]{3,2,0,1:T(8,128)(2,1)}, u32[]{:S(2)}, u32[]{:S(2)}) %all-to-all-start.1) | async-done | bytes 5242912 | tf_op jit(solution)/shard_map/all_to_all | solution.py:90
  108.7 11.5 %fusion.12 = (bf16[1024,896]{0,1:T(8,128)(2,1)S(1)}, bf16[1024,896]{0,1:T(8,128)(2,1)S(1)}, bf16[1024]{0:T(1024)(128)(2,1)S(1)}) fusion(f32[1024]{0:T(1024)S(1)} %reshape.188, bf16[1024,1792]{0,1:T(8,128)(2,1)} %bitcast.126, bf16[1024,2560]{1,0:T(8,128)(2,1)} %bitcast.18, bf16[1,1,896,2560]{3,2,1,0:T(8,128)(2,1)} %all-gather.5.cloned.1.call-done), kind=kOutput, calls=%fused_computation.18 | convolution fusion | flops 4715052032 | bytes 17176576 | tf_op jit(solution)/shard_map/dot_general | solution.py:34
  120.3 0.0 copy-start.4
  120.3 1.2 copy-done.4
  121.5 16.0 %fusion = bf16[1,2560,1792]{1,2,0:T(8,128)(2,1)} fusion(bf16[1,1,1,1024,2560]{4,3,2,1,0:T(8,128)(2,1)} %param.12, bf16[1024,896]{0,1:T(8,128)(2,1)S(1)} %get-tuple-element.31, bf16[1024,896]{0,1:T(8,128)(2,1)S(1)} %get-tuple-element.30), kind=kOutput, calls=%fused_computation.1 | convolution fusion | flops 9407168512 | bytes 18087936 | tf_op jit(solution)/shard_map/erd,erf->edf/dot_general | solution.py:133
  137.4 0.0 reduce-scatter.3.cloned.1.call-update
  137.5 0.0 reduce-scatter.5.cloned.1.call-start
  137.5 11.0 %fusion.7 = bf16[1,896,2560]{2,1,0:T(8,128)(2,1)} fusion(bf16[1024,2560]{1,0:T(8,128)(2,1)} %bitcast.18, f32[1024]{0:T(1024)S(1)} %reshape.188, bf16[1024,1792]{0,1:T(8,128)(2,1)} %bitcast.127), kind=kOutput, calls=%fused_computation.11 | convolution fusion | flops 4708171776 | bytes 13504512 | tf_op jit(solution)/shard_map/erf,erd->efd/dot_general | solution.py:136
  148.6 0.0 reduce-scatter.5.cloned.1.call-update
  148.6 0.7 convert_element_type.125
  149.3 5.3 %all-to-all-start.3 = ((bf16[1,16,64]{2,0,1:T(2,128)(2,1)}), bf16[1,16,64]{2,0,1:T(2,128)(2,1)S(1)}, u32[]{:S(2)}, u32[]{:S(2)}) async-start(bf16[1,16,64]{2,0,1:T(2,128)(2,1)} %convert_element_type.125), calls=%async_computation.3 | async-start | bytes 16384 | tf_op jit(solution)/shard_map/all_to_all | solution.py:111
  154.5 0.0 all-gather.7.cloned.1.call-done
  154.6 15.4 %fusion.3 = bf16[1024,2560]{1,0:T(8,128)(2,1)} fusion(bf16[1,1,2560,1792]{3,2,1,0:T(8,128)(2,1)} %all-gather.7.cloned.1.call-done, bf16[1024,896]{0,1:T(8,128)(2,1)} %copy-done.4, bf16[1024,896]{0,1:T(8,128)(2,1)S(1)} %get-tuple-element.30), kind=kOutput, calls=%fused_computation.5 | convolution fusion | flops 9405202432 | bytes 18087936 | tf_op jit(solution)/shard_map/dot_general | solution.py:44
  170.0 0.0 all-to-all-done.3
  170.0 7.1 %all-to-all-start.2 = ((bf16[1,16,64,2560]{3,2,0,1:T(8,128)(2,1)}), bf16[1,16,64,2560]{3,2,0,1:T(8,128)(2,1)}, u32[]{:S(2)}, u32[]{:S(2)}) async-start(bf16[1,16,64,2560]{3,2,0,1:T(8,128)(2,1)} %bitcast.124), calls=%async_computation.2 | async-start | bytes 10485760 | tf_op jit(solution)/shard_map/all_to_all | solution.py:104
  177.1 0.1 reshape.205
  177.2 73.7 %all-to-all-done.2 = bf16[1,16,64,2560]{3,2,0,1:T(8,128)(2,1)} async-done(((bf16[1,16,64,2560]{3,2,0,1:T(8,128)(2,1)}), bf16[1,16,64,2560]{3,2,0,1:T(8,128)(2,1)}, u32[]{:S(2)}, u32[]{:S(2)}) %all-to-all-start.2) | async-done | bytes 5242912 | tf_op jit(solution)/shard_map/all_to_all | solution.py:104
  250.9 3.5 %fusion.17 = bf16[1,128,2560]{2,1,0:T(8,128)(2,1)S(1)} fusion(bf16[1024,2560]{1,0:T(8,128)(2,1)} %bitcast.24, s32[128]{0:T(128)S(1)} %get-tuple-element.25, s32[128]{0:T(128)S(1)} %get-tuple-element.26, s32[128]{0:T(128)S(1)} %get-tuple-element.27, s32[128]{0:T(128)S(1)} %get-tuple-element.28, s32[128]{0:T(128)S(1)} %get-tuple-element.29, ...), kind=kOutput, calls=%fused_computation.28 | convolution fusion | flops 674562048 | bytes 5901312 | tf_op jit(solution)/shard_map/dot_general | solution.py:121
  254.5 3.7 %collective-permute-start = (bf16[1,128,2560]{2,1,0:T(8,128)(2,1)S(1)}, bf16[1,128,2560]{2,1,0:T(8,128)(2,1)S(1)}, u32[]{:S(2)}, u32[]{:S(2)}) collective-permute-start(bf16[1,128,2560]{2,1,0:T(8,128)(2,1)S(1)} %fusion.17), channel_id=1, source_target_pairs={{16,0},{32,16},{48,32},{0,48},{17,1},{33,17},{49,33},{1,49},{18,2}... | collective-permute-start | bytes 1966088 | tf_op jit(solution)/shard_map/ppermute | solution.py:12
  258.2 0.2 fusion.31
  258.4 0.2 fusion.29
  258.6 0.2 fusion.27
  258.8 0.2 fusion.25
  259.0 0.2 fusion.23
  259.3 0.2 fusion.21
  259.5 0.6 stack.29
  260.1 9.1 %collective-permute-done = bf16[1,128,2560]{2,1,0:T(8,128)(2,1)S(1)} collective-permute-done((bf16[1,128,2560]{2,1,0:T(8,128)(2,1)S(1)}, bf16[1,128,2560]{2,1,0:T(8,128)(2,1)S(1)}, u32[]{:S(2)}, u32[]{:S(2)}) %collective-permute-start) | collective-permute-done | bytes 655392 | tf_op jit(solution)/shard_map/ppermute | solution.py:12
  269.2 0.0 reduce-scatter.3.cloned.1.call-done
  269.2 7.2 %copy.42 = bf16[1,1,1280,1792]{3,2,1,0:T(8,128)(2,1)} copy(bf16[1,1,1280,1792]{2,3,1,0:T(8,128)(2,1)} %bitcast.125) | data formatting | bytes 9175040
  276.4 0.8 copy.46
  277.3 0.0 copy-done.1
  (9 shorter events, 0.1 us)
Async XLA Ops:
  7.2 13.6 %copy-start = (bf16[1,128,2560]{2,1,0:T(8,128)(2,1)S(1)}, bf16[1,128,2560]{2,1,0:T(8,128)(2,1)}, u32[]{:S(2)}) copy-start(bf16[1,128,2560]{2,1,0:T(8,128)(2,1)} %param.7) | copy-start | bytes 1966084
  7.2 1.5 copy-start.2
  7.2 4.5 %copy-start.3 = (bf16[1,128,6]{1,2,0:T(8,128)(2,1)S(1)}, bf16[1,128,6]{1,2,0:T(8,128)(2,1)}, u32[]{:S(2)}) copy-start(bf16[1,128,6]{1,2,0:T(8,128)(2,1)} %param.9) | copy-start | bytes 4612
  7.2 31.9 %all-gather.5.cloned.1.call-start = ((), (), s32[]{:S(2)}) async-start(), calls=%async_computation.8 | async-start | bytes 6881280 | tf_op jit(solution)/shard_map/all_gather | solution.py:62
  7.9 146.6 %all-gather.7.cloned.1.call-start = ((), (), s32[]{:S(2)}) async-start(), calls=%async_computation.9 | async-start | bytes 13762560 | tf_op jit(solution)/shard_map/all_gather | solution.py:61
  13.7 14.6 %all-to-all-start = ((bf16[1,16,64]{2,0,1:T(2,128)(2,1)}), bf16[1,16,64]{2,0,1:T(2,128)(2,1)S(1)}, u32[]{:S(2)}, u32[]{:S(2)}) async-start(bf16[1,16,64]{2,0,1:T(2,128)(2,1)} %reshape.217), calls=%async_computation | async-start | bytes 16384 | tf_op jit(solution)/shard_map/all_to_all | solution.py:91
  28.3 80.5 %all-to-all-start.1 = ((bf16[1,16,64,2560]{3,2,0,1:T(8,128)(2,1)}), bf16[1,16,64,2560]{3,2,0,1:T(8,128)(2,1)}, u32[]{:S(2)}, u32[]{:S(2)}) async-start(bf16[1,16,64,2560]{3,2,0,1:T(8,128)(2,1)} %bitcast.123), calls=%async_computation.1 | async-start | bytes 10485760 | tf_op jit(solution)/shard_map/all_to_all | solution.py:90
  32.9 236.4 %reduce-scatter.3.cloned.1.call-start = ((), (), s32[]{:S(2)}) async-start(), calls=%async_computation.6 | async-start | bytes 13762560 | tf_op jit(solution)/shard_map/reduce_scatter | solution.py:139
  120.3 1.2 copy-start.4
  137.5 139.0 %reduce-scatter.5.cloned.1.call-start = ((), (), s32[]{:S(2)}) async-start(), calls=%async_computation.7 | async-start | bytes 6881280 | tf_op jit(solution)/shard_map/reduce_scatter | solution.py:142
  149.3 20.7 %all-to-all-start.3 = ((bf16[1,16,64]{2,0,1:T(2,128)(2,1)}), bf16[1,16,64]{2,0,1:T(2,128)(2,1)S(1)}, u32[]{:S(2)}, u32[]{:S(2)}) async-start(bf16[1,16,64]{2,0,1:T(2,128)(2,1)} %convert_element_type.125), calls=%async_computation.3 | async-start | bytes 16384 | tf_op jit(solution)/shard_map/all_to_all | solution.py:111
  170.0 80.9 %all-to-all-start.2 = ((bf16[1,16,64,2560]{3,2,0,1:T(8,128)(2,1)}), bf16[1,16,64,2560]{3,2,0,1:T(8,128)(2,1)}, u32[]{:S(2)}, u32[]{:S(2)}) async-start(bf16[1,16,64,2560]{3,2,0,1:T(8,128)(2,1)} %bitcast.124), calls=%async_computation.2 | async-start | bytes 10485760 | tf_op jit(solution)/shard_map/all_to_all | solution.py:104
  254.5 14.7 %collective-permute-start = (bf16[1,128,2560]{2,1,0:T(8,128)(2,1)S(1)}, bf16[1,128,2560]{2,1,0:T(8,128)(2,1)S(1)}, u32[]{:S(2)}, u32[]{:S(2)}) collective-permute-start(bf16[1,128,2560]{2,1,0:T(8,128)(2,1)S(1)} %fusion.17), channel_id=1, source_target_pairs={{16,0},{32,16},{48,32},{0,48},{17,1},{33,17},{49,33},{1,49},{18,2}... | collective-permute-start | bytes 1966088 | tf_op jit(solution)/shard_map/ppermute | solution.py:12
  269.2 8.1 %copy-start.1 = (bf16[1,128,2560]{2,1,0:T(8,128)(2,1)S(1)}, bf16[1,128,2560]{2,1,0:T(8,128)(2,1)}, u32[]{:S(2)}) copy-start(bf16[1,128,2560]{2,1,0:T(8,128)(2,1)} %param.7) | copy-start | bytes 1966084
Sparse Core Ops, SparseCore 0:
  9.7 19.3 all-gather.4
  30.8 25.5 all-gather.6
  137.6 20.4 reduce-scatter.2
  161.0 16.4 reduce-scatter.4
where the time goes:
time: 285 us; the launch traced here: 284 us
  waiting for transfers between devices  157 us (55%)
  matrix products  64.2 us (23%)
  starting transfers between devices  28.1 us (10%)
  local copies, waits for them, and re-layouts  18.5 us (6%)
  between operations  13.9 us (5%)
    all_to_all x1, waiting for transfers between devices, body(): lax.all_to_all(input_grad.reshape(per_device, sources, slot_cap, model_wi...  73.7 us
    all_to_all x1, waiting for transfers between devices, body(): lax.all_to_all(send_grad, 'expert', split_axis=1, concat_axis=1, tiled=True)  69.6 us
    dot_general x1, matrix products, body(): jnp.einsum('erd,erf->edf', expert_in, grad_gu, preferred_element_type=jnp...  16 us
    dot_general x1, matrix products, expert_rows(): lax.dot_general(grad_gu, gate_up, (((1,), (1,)), ((), ())), preferred_ele...  15.4 us
    unnamed x14, local copies, waits for them, and re-layouts  15.4 us
    dot_general x1, matrix products, expert_rows(): lax.dot_general(grad_rows, down_proj, (((1,), (1,)), ((), ())), preferred...  11.5 us
    dot_general x1, matrix products, body(): jnp.einsum('erf,erd->efd', scaled, expert_dy, preferred_element_type=jnp....  11 us
    ppermute x1, waiting for transfers between devices, shifted(): return lax.ppermute(block, axis, route)  9.12 us
  transfers between devices with their start and end apart: 9, of which 4 were waited for; matrix products, arithmetic and copies ran while one was open for 29% of the time, Pallas kernels for 0%

commit v1 on v0

v1 whole, which is shorter than its diff:
```python
import functools

import jax
import jax.numpy as jnp
from jax import lax
from jax.experimental import pallas as pl
from jax.experimental.pallas import tpu as pltpu
from jax.sharding import PartitionSpec as P

SLOT = 64
SIDE = 4
TOK = 128
EXPERTS = 16
MESH = pl.DeviceIdType.MESH
BF = jnp.bfloat16
F32 = jnp.float32
ORDER = (0, 1, 3, 2)


def mod4(i):
    return lax.rem(i, SIDE)


def at(half, u, v):
    return v * SIDE + u if half == 0 else u * SIDE + v


def remote(src, dst, send, recv, **where):
    return pltpu.make_async_remote_copy(
        src_ref=src, dst_ref=dst, send_sem=send, recv_sem=recv, device_id=where, device_id_type=MESH
    )


def enter(**peers):
    barrier = pltpu.get_barrier_semaphore()
    count = 0
    for axis, indices in peers.items():
        for index in indices:
            pl.semaphore_signal(barrier, inc=1, device_id={axis: index}, device_id_type=MESH)
            count += 1
    pl.semaphore_wait(barrier, count)


def one_hot(slots_row):
    ids = lax.broadcasted_iota(jnp.int32, (SLOT, TOK), 0).astype(F32)
    return jnp.where(ids == slots_row, 1.0, 0.0).astype(BF)


def dispatch_kernel(
    tok, routes, combine, wgu, wdn,
    dya, dyb, table, wgu_peer, wdn_peer,
    gathered, staged, relayed, send, recv, table_send, table_recv, dp_send, dp_recv,
):
    me = lax.axis_index("expert")
    dp = lax.axis_index("dp")
    y, x = lax.div(me, SIDE), lax.rem(me, SIDE)
    width = tok.shape[1] // 2
    outs = (dya, dyb)
    uv = ((x, y), (y, x))
    row_peers = [y * SIDE + mod4(x + i) for i in (1, 2, 3)]
    col_peers = [mod4(y + i) * SIDE + x for i in (1, 2, 3)]
    enter(expert=row_peers + col_peers, dp=[1 - dp])
    sends = []

    def go(copy):
        copy.start()
        sends.append(copy)
        return copy

    def ring(half, step):
        u, v = uv[half]
        up, down = at(half, mod4(u + 1), v), at(half, mod4(u + 3), v)
        if step == 0:
            mine = tok.at[:, pl.ds(half * width, width)]
            return (
                remote(mine, gathered.at[half, u], send.at[half, 0], recv.at[half, 0], expert=down),
                remote(mine, gathered.at[half, u], send.at[half, 1], recv.at[half, 1], expert=up),
            )
        first = gathered.at[half, mod4(u + 1), pl.ds(0, TOK // 2)]
        second = gathered.at[half, mod4(u + 3), pl.ds(TOK // 2, TOK // 2)]
        return (
            remote(first, first, send.at[half, 2], recv.at[half, 2], expert=down),
            remote(second, second, send.at[half, 3], recv.at[half, 3], expert=up),
        )

    near = [ring(half, 0) for half in (0, 1)]
    for half in (0, 1):
        for copy in near[half]:
            go(copy)

    ids = lax.broadcasted_iota(jnp.int32, (EXPERTS, TOK), 0)
    chosen = jnp.zeros((EXPERTS, TOK), F32)
    weight = jnp.zeros((EXPERTS, TOK), F32)
    for k in range(routes.shape[0]):
        hit = jnp.where(ids == routes[pl.ds(k, 1), :], 1.0, 0.0)
        chosen = chosen + hit
        weight = weight + hit * combine[pl.ds(k, 1), :]
    before = lax.broadcasted_iota(jnp.int32, (TOK, TOK), 0) < lax.broadcasted_iota(
        jnp.int32, (TOK, TOK), 1
    )
    count = jnp.dot(
        chosen.astype(BF), jnp.where(before, 1.0, 0.0).astype(BF), preferred_element_type=F32
    )
    slots = jnp.where(chosen > 0.5, count, -1.0)
    table[pl.ds(me, 1)] = jnp.concatenate([slots, weight], axis=0)[None]

    row_tables = [
        remote(
            table.at[me], table.at[me], table_send.at[i], table_recv.at[i], expert=row_peers[i]
        )
        for i in range(3)
    ]
    for copy in row_tables:
        go(copy)
    across = [
        remote(wgu, wgu_peer, dp_send.at[0], dp_recv.at[0], dp=1 - dp),
        remote(wdn, wdn_peer, dp_send.at[1], dp_recv.at[1], dp=1 - dp),
    ]
    for copy in across:
        go(copy)

    def deliver(half, r):
        u, v = uv[half]
        source_u = mod4(u + ORDER[r])
        source = at(half, source_u, v)
        maps = [
            one_hot(table[pl.ds(source, 1), pl.ds(at(half, u, mod4(v + j)), 1), :][0])
            for j in range(SIDE)
        ]
        if r == 0:
            block = tok[:, pl.ds(half * width, width)]
        else:
            block = gathered[pl.ds(half, 1), pl.ds(source_u, 1)][0, 0]
        rows = jnp.dot(jnp.concatenate(maps, axis=0), block, preferred_element_type=F32)
        staged[half, r] = rows.astype(BF).reshape(SIDE, SLOT, width)
        up, down = at(half, u, mod4(v + 1)), at(half, u, mod4(v + 3))
        low, high = pl.ds(0, SLOT // 2), pl.ds(SLOT // 2, SLOT // 2)
        out = outs[half]
        i = 12 + 2 * r
        go(remote(staged.at[half, r, 2, low], relayed.at[half, 0, r], send.at[half, i], recv.at[half, i], expert=up))
        go(remote(staged.at[half, r, 2, high], relayed.at[half, 1, r], send.at[half, i + 1], recv.at[half, i + 1], expert=down))
        i = 4 + 2 * r
        go(remote(staged.at[half, r, 1], out.at[source], send.at[half, i], recv.at[half, i], expert=up))
        go(remote(staged.at[half, r, 3], out.at[source], send.at[half, i + 1], recv.at[half, i + 1], expert=down))
        own = pltpu.make_async_copy(staged.at[half, r, 0], out.at[source], send.at[half, 28 + r])
        own.start()
        return own

    def forward(half, r):
        u, v = uv[half]
        source_u = mod4(u + ORDER[r])
        low, high = pl.ds(0, SLOT // 2), pl.ds(SLOT // 2, SLOT // 2)
        up, down = at(half, u, mod4(v + 1)), at(half, u, mod4(v + 3))
        out = outs[half]
        for d, to, part, origin in ((0, up, low, mod4(v + 3)), (1, down, high, mod4(v + 1))):
            slot = relayed.at[half, d, r]
            i = 12 + 2 * r + d
            remote(slot, slot, send.at[half, i], recv.at[half, i], expert=to).wait_recv()
            i = 20 + 2 * r + d
            go(remote(slot, out.at[at(half, source_u, origin), part], send.at[half, i], recv.at[half, i], expert=to))

    owns = [deliver(half, 0) for half in (0, 1)]
    for copy in row_tables:
        copy.wait_recv()
    mine = pl.ds(y * SIDE, SIDE)
    col_tables = [
        remote(
            table.at[mine], table.at[mine], table_send.at[3 + i], table_recv.at[3 + i], expert=col_peers[i]
        )
        for i in range(3)
    ]
    for copy in col_tables:
        go(copy)
    for half in (0, 1):
        for copy in near[half]:
            copy.wait_recv()
        for copy in ring(half, 1):
            go(copy)
    for copy in col_tables:
        copy.wait_recv()
    for r in (1, 2):
        for half in (0, 1):
            owns.append(deliver(half, r))
            forward(half, r - 1)
    for half in (0, 1):
        for copy in ring(half, 1):
            copy.wait_recv()
        owns.append(deliver(half, 3))
    for r in (2, 3):
        for half in (0, 1):
            forward(half, r)
    for half in (0, 1):
        for r in range(SIDE):
            for d in (0, 1):
                low = pl.ds(0, SLOT // 2)
                for i, piece in ((4 + 2 * r + d, outs[half].at[0]), (20 + 2 * r + d, outs[half].at[0, low])):
                    remote(piece, piece, send.at[half, i], recv.at[half, i], expert=me).wait_recv()
    for copy in owns:
        copy.wait()
    for copy in across:
        copy.wait_recv()
    for copy in sends:
        copy.wait_send()


def dispatch(tok, routes, combine, wgu, wdn):
    width = tok.shape[1] // 2
    vmem = pl.BlockSpec(memory_space=pltpu.VMEM)
    anyw = pl.BlockSpec(memory_space=pl.ANY)
    block = jax.ShapeDtypeStruct((EXPERTS, SLOT, width), BF)
    return pl.pallas_call(
        dispatch_kernel,
        out_shape=(
            block,
            block,
            jax.ShapeDtypeStruct((EXPERTS, 2 * EXPERTS, TOK), F32),
            jax.ShapeDtypeStruct(wgu.shape, BF),
            jax.ShapeDtypeStruct(wdn.shape, BF),
        ),
        in_specs=[vmem, vmem, vmem, anyw, anyw],
        out_specs=(anyw, anyw, vmem, anyw, anyw),
        scratch_shapes=[
            pltpu.VMEM((2, SIDE, TOK, width), BF),
            pltpu.VMEM((2, SIDE, SIDE, SLOT, width), BF),
            pltpu.VMEM((2, 2, SIDE, SLOT // 2, width), BF),
            pltpu.SemaphoreType.DMA((2, 32)),
            pltpu.SemaphoreType.DMA((2, 32)),
            pltpu.SemaphoreType.DMA((6,)),
            pltpu.SemaphoreType.DMA((6,)),
            pltpu.SemaphoreType.DMA((2,)),
            pltpu.SemaphoreType.DMA((2,)),
        ],
        compiler_params=pltpu.CompilerParams(
            collective_id=0, has_side_effects=True, vmem_limit_bytes=40 * 1024 * 1024
        ),
        name="dispatch",
    )(tok, routes, combine, wgu, wdn)


def rounded(values):
    return lax.optimization_barrier(values.astype(jnp.bfloat16)).astype(jnp.float32)


def shifted(block, axis, distance):
    devices = range(lax.axis_size(axis))
    route = [((i - distance) % len(devices), i) for i in devices]
    return lax.ppermute(block, axis, route)


def body(out_grad, routes, combine, gate_up_weight, down_weight, saved_inputs, saved_gate_up):
    me = lax.axis_index("expert")
    dp = lax.axis_index("dp")
    rt, cb = routes[0].T, combine[0].T.astype(F32)
    dya, dyb, table, wgu_peer, wdn_peer = dispatch(out_grad[0], rt, cb, gate_up_weight[0, 0], down_weight[0, 0])
    first = dp == 0
    own_gu, own_dn = gate_up_weight[0, 0], down_weight[0, 0]
    gate_up = jnp.concatenate([jnp.where(first, own_gu, wgu_peer), jnp.where(first, wgu_peer, own_gu)], axis=0)
    down_proj = jnp.concatenate([jnp.where(first, own_dn, wdn_peer), jnp.where(first, wdn_peer, own_dn)], axis=1)
    dy = jnp.concatenate([dya, dyb], axis=2).reshape(1024, -1)
    ids = jnp.arange(SLOT, dtype=F32)
    s_all, w_all = table[:, :EXPERTS], table[:, EXPERTS:]
    s_me = lax.dynamic_index_in_dim(s_all, me, 1, keepdims=False)
    w_me = lax.dynamic_index_in_dim(w_all, me, 1, keepdims=False)
    weight_rows = jnp.sum(jnp.where(ids[None, :, None] == s_me[:, None, :], w_me[:, None, :], 0.0), axis=2).reshape(-1)
    gu_rows = saved_gate_up[0, 0, 0]
    ff = gu_rows.shape[1] // 2
    gate_pre = gu_rows[:, :ff].astype(F32)
    up_pre = gu_rows[:, ff:].astype(F32)
    logistic = jax.nn.sigmoid(gate_pre)
    activated = gate_pre * logistic
    hidden = activated * up_pre
    through = lax.dot_general(dy, down_proj, (((1,), (1,)), ((), ())), preferred_element_type=F32)
    comb_part = jnp.sum(through * hidden, axis=1).astype(BF)
    factor = weight_rows[:, None]
    scaled = (factor * hidden).astype(BF)
    grad_hidden = factor * through
    grad_gate = grad_hidden * up_pre * logistic * (1.0 + gate_pre * (1.0 - logistic))
    grad_up = grad_hidden * activated
    grad_gu = jnp.concatenate([grad_gate, grad_up], axis=1).astype(BF)
    input_grad = lax.dot_general(grad_gu, gate_up, (((1,), (1,)), ((), ())), preferred_element_type=F32).astype(BF)
    back = lax.all_to_all(input_grad.reshape(1, 16, SLOT, -1), "expert", split_axis=1, concat_axis=1, tiled=True)
    comb = lax.all_to_all(comb_part.reshape(1, 16, SLOT), "expert", split_axis=1, concat_axis=1, tiled=True)[0]
    s_own = lax.dynamic_index_in_dim(s_all, me, 0, keepdims=False)
    onehot = (ids[None, :, None] == s_own[:, None, :]).astype(BF).reshape(1024, TOK)
    layer = lax.dot_general(onehot, back.reshape(1024, -1), (((0,), (0,)), ((), ())), preferred_element_type=F32).astype(BF)
    passed = shifted(layer[None], "pipe", -1)
    comb_et = jnp.sum(onehot.reshape(16, SLOT, TOK).astype(F32) * comb[:, :, None].astype(F32), axis=1)
    comb_grad = jnp.sum(jnp.where(rt[:, None, :] == jnp.arange(16)[None, :, None], comb_et[None], 0.0), axis=1).T.astype(BF)[None]
    part_gu = jnp.einsum("rd,rf->df", saved_inputs[0, 0, 0], grad_gu, preferred_element_type=F32).astype(BF)
    part_dn = jnp.einsum("rf,rd->fd", scaled, dy, preferred_element_type=F32).astype(BF)
    sum_gu = lax.psum_scatter(part_gu, "dp", scatter_dimension=0, tiled=True)
    sum_dn = lax.psum_scatter(part_dn, "dp", scatter_dimension=1, tiled=True)
    return passed, comb_grad, sum_gu[None, None], sum_dn[None, None]


def solution(mesh):
    placed = (
        P("pipe", ("dp", "expert"), None),
        P("pipe", ("dp", "expert"), None),
        P("pipe", ("dp", "expert"), None),
        P("pipe", "expert", "dp", None),
        P("pipe", "expert", None, "dp"),
        P("pipe", "dp", "expert", None, None),
        P("pipe", "dp", "expert", None, None),
    )
    return jax.shard_map(
        body,
        mesh=mesh,
        in_specs=placed,
        out_specs=(
            P("pipe", ("dp", "expert"), None),
            P("pipe", ("dp", "expert"), None),
            P("pipe", "expert", "dp", None),
            P("pipe", "expert", None, "dp"),
        ),
        check_vma=False,
    )
```

time: 285 us -> 250 us (0.88)
  waiting for transfers between devices: 157 us -> 77 us
  Pallas kernels: 0 us -> 49.4 us
  starting transfers between devices: 28.1 us -> 8.02 us
  matrix products: 64.2 us -> 49.4 us
  blocking collectives: 0 us -> 12.5 us
  other arithmetic: 1.93 us -> 13 us
  local copies, waits for them, and re-layouts: 18.5 us -> 25.8 us
    all_to_all x4 -> x1, waiting for transfers between devices: 147 us -> 77 us  [body(): lax.all_to_all(input_grad.reshape(1, 16, SLOT, -1), 'expert', split_axis=...]
    pallas_call x0 -> x1, Pallas kernels: none -> 49.4 us  [dispatch(): pl.pallas_call(dispatch_kernel, out_shape=(block, block, jax.ShapeDtypeSt...]
    all_to_all x4 -> x1, starting transfers between devices: 24.1 us -> 4.72 us  [body(): lax.all_to_all(input_grad.reshape(1, 16, SLOT, -1), 'expert', split_axis=...]
    dot_general x18 -> x5, matrix products: 64.2 us -> 49.4 us  [the longest x1 14.1 us: body(): lax.dot_general(grad_gu, gate_up, (((1,), (1,)), ((), ())), preferred_ele...]
    all_to_all x0 -> x1, blocking collectives: none -> 12.5 us  [body(): lax.all_to_all(comb_part.reshape(1, 16, SLOT), 'expert', split_axis=1, co...]
    unnamed x14 -> x28, local copies, waits for them, and re-layouts: 15.4 us -> 25.6 us
    ppermute x1, waiting for transfers between devices: 9.12 us -> 0.01 us  [shifted(): return lax.ppermute(block, axis, route)]
    select_n x0 -> x2, other arithmetic: none -> 8.81 us  [the longest x1 8.51 us: body(): jnp.where(first, own_gu, wgu_peer)]
  transfers between devices with their start and end apart: 9 -> 4, of which waited for: 4 -> 1; matrix products, arithmetic and copies ran while one was open for 29% -> 18% of each run, Pallas kernels for 0% -> 0%
where the time goes in v1:
time: 250 us; the launch traced here: 249 us
  waiting for transfers between devices  77 us (31%)
  Pallas kernels  49.4 us (20%)
  matrix products  49.4 us (20%)
  local copies, waits for them, and re-layouts  25.8 us (10%)
  between operations  14.2 us (6%)
  other arithmetic  13 us (5%)
  blocking collectives  12.5 us (5%)
  starting transfers between devices  8.02 us (3%)
    all_to_all x1, waiting for transfers between devices, body(): lax.all_to_all(input_grad.reshape(1, 16, SLOT, -1), 'expert', split_axis=...  77 us
    pallas_call x1, Pallas kernels, dispatch(): pl.pallas_call(dispatch_kernel, out_shape=(block, block, jax.ShapeDtypeSt...  49.4 us
    unnamed x28, local copies, waits for them, and re-layouts  25.6 us
    dot_general x1, matrix products, body(): lax.dot_general(grad_gu, gate_up, (((1,), (1,)), ((), ())), preferred_ele...  14.1 us
    dot_general x1, matrix products, body(): jnp.einsum('rd,rf->df', saved_inputs[0, 0, 0], grad_gu, preferred_element...  13.8 us
    all_to_all x1, blocking collectives, body(): lax.all_to_all(comb_part.reshape(1, 16, SLOT), 'expert', split_axis=1, co...  12.5 us
    dot_general x1, matrix products, body(): jnp.einsum('rf,rd->fd', scaled, dy, preferred_element_type=F32).astype(BF)  11.3 us
    select_n x1, other arithmetic, body(): jnp.where(first, own_gu, wgu_peer)  8.51 us
  transfers between devices with their start and end apart: 4, of which 1 were waited for; matrix products, arithmetic and copies ran while one was open for 18% of the time, Pallas kernels for 0%

profile of v1, /device:TPU:0, one launch (start us, length us, event | category | flops | bytes accessed | tf_op | source)
XLA Modules:
  0.0 249.4 jit_solution(7129882191219074990)
XLA Ops:
  7.2 0.0 reduce-scatter.3.cloned.1.call-start
  7.2 0.7 copy.26
  7.9 0.7 convert_bitcast_fusion.combine
  8.6 0.0 copy-start
  8.6 1.6 copy-done
  10.2 0.0 copy-start.5
  10.2 1.1 copy-done.5
  11.3 49.4 %dispatch.1 = (bf16[16,64,1280]{2,1,0:T(8,128)(2,1)S(1)}, bf16[16,64,1280]{2,1,0:T(8,128)(2,1)S(1)}, f32[16,32,128]{2,1,0:T(8,128)S(1)}, bf16[1280,1792]{1,0:T(8,128)(2,1)}, bf16[896,1280]{1,0:T(8,128)(2,1)S(1)}) custom-call(bf16[128,2560]{1,0:T(8,128)(2,1)S(1)} %bitcast.48, s32[6,128]{1,0:T(8,128)S(1)} %bitcast.49, ...), custom_call_target="tpu_custom_call" | custom-call | tf_op jit(solution)/shard_map/dispatch/pallas_call | solution.py:211
  60.7 0.0 copy-start.2
  60.7 1.5 copy-done.2
  62.3 0.0 copy-start.3
  62.3 1.4 copy-done.3
  63.7 0.2 select_reduce_fusion
  63.9 0.1 mul.48
  64.0 5.9 %copy.20 = bf16[1,1,1,1024,1792]{3,4,2,1,0:T(8,128)(2,1)} copy(bf16[1,1,1,1024,1792]{4,3,2,1,0:T(8,128)(2,1)} %param.13) | data formatting | bytes 7340032 | tf_op args[6]
  69.9 0.0 copy-start.1
  69.9 0.0 copy-start.4
  69.9 2.4 pad_maximum_fusion
  72.3 0.0 copy-start.6
  72.3 0.1 copy-done.1
  72.4 0.7 copy-done.4
  73.0 0.0 copy-start.7
  73.1 0.0 slice-start
  73.1 0.3 broadcast_select_fusion.3
  73.4 1.3 copy-done.6
  74.7 1.5 copy-done.7
  76.2 0.0 slice-start.1
  76.2 6.9 %fusion.15 = (bf16[1024,896]{0,1:T(8,128)(2,1)S(1)}, bf16[1024,896]{0,1:T(8,128)(2,1)S(1)}, bf16[1024]{0:T(1024)(128)(2,1)S(1)}) fusion(f32[1024]{0:T(1024)S(1)} %mul.48, bf16[1024,1792]{0,1:T(8,128)(2,1)S(1)} %bitcast.57, bf16[1024,2560]{1,0:T(8,128)(2,1)S(1)} %bitcast.52, bf16[896,1280]{1,0:T(8,128)(2,1)S(1)} %get-tuple-element.36, ...), kind=kOutput, calls=%fused_computation.23 | convolution fusion | flops 4724227072 | bytes 17176576 | tf_op jit(solution)/shard_map/dot_general | solution.py:272
  83.1 0.0 copy-start.8
  83.1 0.0 copy-start.9
  83.1 1.3 copy-done.8
  84.4 0.5 copy-done.9
  84.9 0.0 slice-done
  84.9 0.0 slice-done.1
  84.9 13.8 %fusion = bf16[2560,1792]{0,1:T(8,128)(2,1)} fusion(bf16[1,1,1,1024,2560]{4,3,2,1,0:T(8,128)(2,1)S(1)} %bitcast.64, bf16[1024,896]{0,1:T(8,128)(2,1)S(1)} %get-tuple-element.33, bf16[1024,896]{0,1:T(8,128)(2,1)S(1)} %get-tuple-element.32), kind=kOutput, calls=%fused_computation.1 | convolution fusion | flops 9407168512 | bytes 18087936 | tf_op jit(solution)/shard_map/rd,rf->df/dot_general | solution.py:289
  98.7 0.0 reduce-scatter.3.cloned.1.call-update
  98.7 0.2 reduce-scatter.5.cloned.1.call-start
  98.9 11.3 %convolution_convert_fusion.1 = bf16[896,2560]{1,0:T(8,128)(2,1)} fusion(bf16[1024,2560]{1,0:T(8,128)(2,1)} %bitcast.53, f32[1024]{0:T(1024)S(1)} %mul.48, bf16[1024,1792]{0,1:T(8,128)(2,1)} %bitcast.56), kind=kOutput, calls=%fused_computation.10 | convolution fusion | flops 4708171776 | bytes 13504512 | tf_op jit(solution)/shard_map/rf,rd->fd/dot_general | solution.py:290
  110.2 0.0 reduce-scatter.5.cloned.1.call-update
  110.2 8.5 %broadcast_select_fusion.1 = (bf16[1280,1792]{1,0:T(8,128)(2,1)S(1)}, bf16[1280,1792]{1,0:T(8,128)(2,1)}) fusion(bf16[1280,1792]{1,0:T(8,128)(2,1)} %get-tuple-element.13, pred[]{:T(512)S(6)} %eq.65, bf16[1,1,1280,1792]{3,2,1,0:T(8,128)(2,1)} %param.10), kind=kLoop, calls=%fused_computation.18 | loop fusion | flops 4587520 | bytes 18350080 | tf_op jit(solution)/shard_map/jit(_where)/select_n | solution.py:257
  118.8 14.1 %fusion.5 = bf16[1024,2560]{1,0:T(8,128)(2,1)} fusion(bf16[1280,1792]{1,0:T(8,128)(2,1)} %get-tuple-element.31, bf16[1280,1792]{1,0:T(8,128)(2,1)S(1)} %get-tuple-element.30, bf16[1024,896]{0,1:T(8,128)(2,1)} %copy-done.9, bf16[1024,896]{0,1:T(8,128)(2,1)} %copy-done.8), kind=kOutput, calls=%fused_computation.6 | convolution fusion | flops 9423552512 | bytes 18087936 | tf_op jit(solution)/shard_map/dot_general | solution.py:280
  132.8 4.7 %all-to-all-start = ((bf16[1,16,64,2560]{3,2,0,1:T(8,128)(2,1)}), bf16[1,16,64,2560]{3,2,0,1:T(8,128)(2,1)}, u32[]{:S(2)}, u32[]{:S(2)}) async-start(bf16[1,16,64,2560]{3,2,0,1:T(8,128)(2,1)} %bitcast.54), calls=%async_computation | async-start | bytes 10485760 | tf_op jit(solution)/shard_map/all_to_all | solution.py:281
  137.6 0.1 iota_compare_fusion.1
  137.7 77.0 %all-to-all-done = bf16[1,16,64,2560]{3,2,0,1:T(8,128)(2,1)} async-done(((bf16[1,16,64,2560]{3,2,0,1:T(8,128)(2,1)}), bf16[1,16,64,2560]{3,2,0,1:T(8,128)(2,1)}, u32[]{:S(2)}, u32[]{:S(2)}) %all-to-all-start) | async-done | bytes 5242912 | tf_op jit(solution)/shard_map/all_to_all | solution.py:281
  214.7 3.4 %fusion.20 = bf16[1,128,2560]{2,1,0:T(8,128)(2,1)S(1)} fusion(pred[1024,128]{1,0:T(32,128)(4,1)S(1)} %bitcast.58, bf16[1024,2560]{1,0:T(8,128)(2,1)} %bitcast.14), kind=kOutput, calls=%fused_computation.33 | convolution fusion | flops 671416320 | bytes 6029312 | tf_op jit(solution)/shard_map/dot_general | solution.py:285
  218.1 3.0 %collective-permute-start = (bf16[1,128,2560]{2,1,0:T(8,128)(2,1)S(1)}, bf16[1,128,2560]{2,1,0:T(8,128)(2,1)S(1)}, u32[]{:S(2)}, u32[]{:S(2)}) collective-permute-start(bf16[1,128,2560]{2,1,0:T(8,128)(2,1)S(1)} %fusion.20), channel_id=1, source_target_pairs={{16,0},{32,16},{48,32},{0,48},{17,1},{33,17},{49,33},{1,49},{18,2}... | collective-permute-start | bytes 1966088 | tf_op jit(solution)/shard_map/ppermute | solution.py:247
  221.1 0.1 convert_element_type.90
  221.2 12.5 %all_to_all.10 = bf16[1,16,64]{2,0,1:T(2,128)(2,1)S(1)} all-to-all(bf16[1,16,64]{2,0,1:T(2,128)(2,1)S(1)} %convert_element_type.90), channel_id=1, replica_groups=mesh['dp'=2,'pipe'=4,'expert'=16] {'expert'}, dimensions={1} | all-to-all | bytes 4096 | tf_op jit(solution)/shard_map/all_to_all | solution.py:282
  233.7 0.2 multiply_reduce_fusion.1
  233.9 0.6 select_reduce_fusion.1
  234.5 0.0 collective-permute-done
  234.5 0.0 reduce-scatter.3.cloned.1.call-done
  234.6 7.2 %copy.23 = bf16[1,1,1280,1792]{3,2,1,0:T(8,128)(2,1)} copy(bf16[1,1,1280,1792]{2,3,1,0:T(8,128)(2,1)} %bitcast.55) | data formatting | bytes 9175040
  241.7 0.0 reduce-scatter.5.cloned.1.call-done
  241.7 0.8 copy.30
  (5 shorter events, 0.1 us)
Async XLA Ops:
  7.2 227.4 %reduce-scatter.3.cloned.1.call-start = ((), (), s32[]{:S(2)}) async-start(), calls=%async_computation.4 | async-start | bytes 13762560 | tf_op jit(solution)/shard_map/reduce_scatter | solution.py:291
  8.6 1.6 copy-start
  10.2 1.1 copy-start.5
  60.7 1.5 copy-start.2
  62.3 1.4 copy-start.3
  69.9 2.4 copy-start.1
  69.9 3.1 %copy-start.4 = (bf16[896,1280]{1,0:T(8,128)(2,1)S(1)}, bf16[896,1280]{1,0:T(8,128)(2,1)}, u32[]{:S(2)}) copy-start(bf16[896,1280]{1,0:T(8,128)(2,1)} %copy-done.3) | copy-start | bytes 6881284
  72.3 2.4 copy-start.6
  73.0 3.1 %copy-start.7 = (bf16[1,1,1,1024,1792]{3,4,2,1,0:T(8,128)(2,1)S(1)}, bf16[1,1,1,1024,1792]{3,4,2,1,0:T(8,128)(2,1)}, u32[]{:S(2)}) copy-start(bf16[1,1,1,1024,1792]{3,4,2,1,0:T(8,128)(2,1)} %copy.20) | copy-start | bytes 11010052
  73.1 11.8 %slice-start = ((s8[5242880]{0:T(1024)(128)(4,1)}), s8[1048576]{0:T(1024)(128)(4,1)S(1)}, s32[]{:S(2)}) async-start(s8[5242880]{0:T(1024)(128)(4,1)} %bitcast.63), calls=%async_computation.6 | async-start | bytes 2097152
  76.2 8.7 %slice-start.1 = ((s8[5242880]{0:T(1024)(128)(4,1)}), s8[4194304]{0:T(1024)(128)(4,1)S(1)}, s32[]{:S(2)}) async-start(s8[5242880]{0:T(1024)(128)(4,1)} %bitcast.63), calls=%async_computation.7 | async-start | bytes 8388608
  83.1 1.3 copy-start.8
  83.1 1.8 copy-start.9
  98.7 143.0 %reduce-scatter.5.cloned.1.call-start = ((), (), s32[]{:S(2)}) async-start(), calls=%async_computation.5 | async-start | bytes 6881280 | tf_op jit(solution)/shard_map/reduce_scatter | solution.py:292
  132.8 81.8 %all-to-all-start = ((bf16[1,16,64,2560]{3,2,0,1:T(8,128)(2,1)}), bf16[1,16,64,2560]{3,2,0,1:T(8,128)(2,1)}, u32[]{:S(2)}, u32[]{:S(2)}) async-start(bf16[1,16,64,2560]{3,2,0,1:T(8,128)(2,1)} %bitcast.54), calls=%async_computation | async-start | bytes 10485760 | tf_op jit(solution)/shard_map/all_to_all | solution.py:281
  218.1 16.5 %collective-permute-start = (bf16[1,128,2560]{2,1,0:T(8,128)(2,1)S(1)}, bf16[1,128,2560]{2,1,0:T(8,128)(2,1)S(1)}, u32[]{:S(2)}, u32[]{:S(2)}) collective-permute-start(bf16[1,128,2560]{2,1,0:T(8,128)(2,1)S(1)} %fusion.20), channel_id=1, source_target_pairs={{16,0},{32,16},{48,32},{0,48},{17,1},{33,17},{49,33},{1,49},{18,2}... | collective-permute-start | bytes 1966088 | tf_op jit(solution)/shard_map/ppermute | solution.py:247
Sparse Core Ops, SparseCore 0:
  98.8 19.8 reduce-scatter.2
  121.7 16.5 reduce-scatter.4

commit v2 on v1

--- a/solution.py
+++ b/solution.py
@@ -15,6 +15,8 @@
 BF = jnp.bfloat16
 F32 = jnp.float32
 ORDER = (0, 1, 3, 2)
+CHUNKS = ((0, 768), (768, 512))
+DN_CUTS = ((0, 384), (384, 512))
 
 
 def mod4(i):
@@ -47,9 +49,10 @@
 
 
 def dispatch_kernel(
-    tok, routes, combine, wgu, wdn,
-    dya, dyb, table, wgu_peer, wdn_peer,
-    gathered, staged, relayed, send, recv, table_send, table_recv, dp_send, dp_recv,
+    tok, routes, combine, wgu, wdn, saved,
+    dya, dyb, table, wgu_peer, wdn_peer, coef_out, hidden_out, scaled_out,
+    gathered, staged, relayed, held, coef, hidden, scaled,
+    send, recv, table_send, table_recv, dp_send, dp_recv, load_sem, store_sem,
 ):
     me = lax.axis_index("expert")
     dp = lax.axis_index("dp")
@@ -59,6 +62,8 @@
     uv = ((x, y), (y, x))
     row_peers = [y * SIDE + mod4(x + i) for i in (1, 2, 3)]
     col_peers = [mod4(y + i) * SIDE + x for i in (1, 2, 3)]
+    load = pltpu.make_async_copy(saved, held, load_sem)
+    load.start()
     enter(expert=row_peers + col_peers, dp=[1 - dp])
     sends = []
 
@@ -158,6 +163,35 @@
             remote(slot, slot, send.at[half, i], recv.at[half, i], expert=to).wait_recv()
             i = 20 + 2 * r + d
             go(remote(slot, out.at[at(half, source_u, origin), part], send.at[half, i], recv.at[half, i], expert=to))
+
+    ff = hidden.shape[1]
+    stores = []
+
+    def prepare(quarter):
+        @pl.loop(0, SIDE)
+        def _(i):
+            source = quarter * SIDE + i
+            rows = pl.ds(pl.multiple_of(source * SLOT, SLOT), SLOT)
+            mine = table[pl.ds(source, 1), pl.ds(me, 1), :][0]
+            given = table[pl.ds(source, 1), pl.ds(EXPERTS + me, 1), :][0]
+            ids = lax.broadcasted_iota(jnp.int32, (SLOT, TOK), 0).astype(F32)
+            factor = jnp.sum(jnp.where(ids == mine, given, 0.0), axis=1, keepdims=True)
+            gate = held[rows, pl.ds(0, ff)].astype(F32)
+            up = held[rows, pl.ds(ff, ff)].astype(F32)
+            logistic = 1.0 / (1.0 + jnp.exp(-gate))
+            active = gate * logistic
+            value = active * up
+            hidden[rows, :] = value
+            scaled[rows, :] = (factor * value).astype(BF)
+            slope = up * logistic * (1.0 + gate * (1.0 - logistic))
+            coef[rows, pl.ds(0, ff)] = factor * slope
+            coef[rows, pl.ds(ff, ff)] = factor * active
+
+        rows = pl.ds(quarter * SIDE * SLOT, SIDE * SLOT)
+        for i, (src, dst) in enumerate(((coef, coef_out), (hidden, hidden_out), (scaled, scaled_out))):
+            copy = pltpu.make_async_copy(src.at[rows], dst.at[rows], store_sem.at[quarter, i])
+            copy.start()
+            stores.append(copy)
 
     owns = [deliver(half, 0) for half in (0, 1)]
     for copy in row_tables:
@@ -186,16 +220,21 @@
         for copy in ring(half, 1):
             copy.wait_recv()
         owns.append(deliver(half, 3))
-    for r in (2, 3):
-        for half in (0, 1):
-            forward(half, r)
+    load.wait()
+    prepare(0)
+    for half in (0, 1):
+        forward(half, 2)
+    for quarter in (1, 2, 3):
+        prepare(quarter)
+    for half in (0, 1):
+        forward(half, 3)
     for half in (0, 1):
         for r in range(SIDE):
             for d in (0, 1):
                 low = pl.ds(0, SLOT // 2)
                 for i, piece in ((4 + 2 * r + d, outs[half].at[0]), (20 + 2 * r + d, outs[half].at[0, low])):
                     remote(piece, piece, send.at[half, i], recv.at[half, i], expert=me).wait_recv()
-    for copy in owns:
+    for copy in owns + stores:
         copy.wait()
     for copy in across:
         copy.wait_recv()
@@ -203,10 +242,11 @@
         copy.wait_send()
 
 
-def dispatch(tok, routes, combine, wgu, wdn):
+def dispatch(tok, routes, combine, wgu, wdn, saved):
+    rows, both = saved.shape
     width = tok.shape[1] // 2
     vmem = pl.BlockSpec(memory_space=pltpu.VMEM)
-    anyw = pl.BlockSpec(memory_space=pl.ANY)
+    anyw = pl.BlockSpec(memory_space=pltpu.HBM)
     block = jax.ShapeDtypeStruct((EXPERTS, SLOT, width), BF)
     return pl.pallas_call(
         dispatch_kernel,
@@ -216,81 +256,414 @@
             jax.ShapeDtypeStruct((EXPERTS, 2 * EXPERTS, TOK), F32),
             jax.ShapeDtypeStruct(wgu.shape, BF),
             jax.ShapeDtypeStruct(wdn.shape, BF),
+            jax.ShapeDtypeStruct((rows, both), F32),
+            jax.ShapeDtypeStruct((rows, both // 2), F32),
+            jax.ShapeDtypeStruct((rows, both // 2), BF),
         ),
-        in_specs=[vmem, vmem, vmem, anyw, anyw],
-        out_specs=(anyw, anyw, vmem, anyw, anyw),
+        in_specs=[vmem, vmem, vmem, anyw, anyw, anyw],
+        out_specs=(anyw, anyw, vmem, anyw, anyw, anyw, anyw, anyw),
         scratch_shapes=[
             pltpu.VMEM((2, SIDE, TOK, width), BF),
             pltpu.VMEM((2, SIDE, SIDE, SLOT, width), BF),
             pltpu.VMEM((2, 2, SIDE, SLOT // 2, width), BF),
+            pltpu.VMEM((rows, both), BF),
+            pltpu.VMEM((rows, both), F32),
+            pltpu.VMEM((rows, both // 2), F32),
+            pltpu.VMEM((rows, both // 2), BF),
             pltpu.SemaphoreType.DMA((2, 32)),
             pltpu.SemaphoreType.DMA((2, 32)),
             pltpu.SemaphoreType.DMA((6,)),
             pltpu.SemaphoreType.DMA((6,)),
             pltpu.SemaphoreType.DMA((2,)),
             pltpu.SemaphoreType.DMA((2,)),
+            pltpu.SemaphoreType.DMA,
+            pltpu.SemaphoreType.DMA((SIDE, 3)),
         ],
         compiler_params=pltpu.CompilerParams(
-            collective_id=0, has_side_effects=True, vmem_limit_bytes=40 * 1024 * 1024
+            collective_id=0, has_side_effects=True, vmem_limit_bytes=62 * 1024 * 1024
         ),
         name="dispatch",
-    )(tok, routes, combine, wgu, wdn)
-
-
-def rounded(values):
-    return lax.optimization_barrier(values.astype(jnp.bfloat16)).astype(jnp.float32)
-
-
-def shifted(block, axis, distance):
-    devices = range(lax.axis_size(axis))
-    route = [((i - distance) % len(devices), i) for i in devices]
-    return lax.ppermute(block, axis, route)
-
-
-def body(out_grad, routes, combine, gate_up_weight, down_weight, saved_inputs, saved_gate_up):
+    )(tok, routes, combine, wgu, wdn, saved)
+
+
+def contract(a, b, da, db):
+    return lax.dot_general(a, b, (((da,), (db,)), ((), ())), preferred_element_type=F32)
+
+
+def backward_kernel(
+    dya, dyb, table, wgu_own, wgu_peer, wdn_own, wdn_peer, coef_in, hidden_in, scaled_in, inputs,
+    passed, comb_in, gu_own, gu_recv, dn_own, dn_recv,
+    wgu, wdn, dy, saved, scaled, coef, hidden, grad,
+    outgoing, returned, relayed, partial, sending, half_in, full_in, final,
+    comb_out, comb_mid, gu_stage, dn_stage,
+    load_sem, part_sem, send, recv, comb_send, comb_recv, dw_send, dw_recv, own_sem,
+):
     me = lax.axis_index("expert")
     dp = lax.axis_index("dp")
+    pipe = lax.axis_index("pipe")
+    y, x = lax.div(me, SIDE), lax.rem(me, SIDE)
+    width = dy.shape[-1]
+    ff = hidden.shape[-1]
+    uv = ((x, y), (y, x))
+    row_peers = [y * SIDE + mod4(x + i) for i in (1, 2, 3)]
+    col_peers = [mod4(y + i) * SIDE + x for i in (1, 2, 3)]
+    chunks = CHUNKS
+    group = SIDE * SLOT
+
+    loads = {}
+
+    def load(name, src, dst, sem):
+        loads[name] = pltpu.make_async_copy(src, dst, sem)
+        loads[name].start()
+
+    def stream(q):
+        rows = pl.ds(q * group, group)
+        load(("coef", q), coef_in.at[rows], coef.at[q % 2], part_sem.at[q, 0])
+        load(("hidden", q), hidden_in.at[rows], hidden.at[q % 2], part_sem.at[q, 1])
+
+    load("wdn_own", wdn_own, wdn.at[dp], load_sem.at[0])
+    load("wdn_peer", wdn_peer, wdn.at[1 - dp], load_sem.at[1])
+    load("dya", dya, dy.at[0], load_sem.at[2])
+    load("dyb", dyb, dy.at[1], load_sem.at[3])
+    stream(0)
+    stream(1)
+    load("wgu_own", wgu_own, wgu.at[dp], load_sem.at[4])
+    load("wgu_peer", wgu_peer, wgu.at[1 - dp], load_sem.at[5])
+    load("scaled", scaled_in, scaled, load_sem.at[6])
+    load("in0", inputs.at[:, pl.ds(0, width)], saved.at[0], load_sem.at[7])
+    load("in1", inputs.at[:, pl.ds(width, width)], saved.at[1], load_sem.at[8])
+    enter(
+        expert=row_peers + col_peers,
+        dp=[1 - dp],
+        pipe=[mod4(pipe + 1), mod4(pipe + 3)],
+    )
+    sends = []
+
+    def go(copy):
+        copy.start()
+        sends.append(copy)
+        return copy
+
+    for name in ("wdn_own", "wdn_peer", "dya", "dyb"):
+        loads[name].wait()
+    for q in range(SIDE):
+        loads[("coef", q)].wait()
+        loads[("hidden", q)].wait()
+        sources = pl.ds(q * SIDE, SIDE)
+        through = contract(dy[0, sources].reshape(group, width), wdn[0], 1, 1) + contract(
+            dy[1, sources].reshape(group, width), wdn[1], 1, 1
+        )
+        comb = jnp.sum(through * hidden[q % 2], axis=1, keepdims=True).astype(BF).astype(F32)
+        factor = coef[q % 2]
+        grad[q, :, :, pl.ds(0, ff)] = (through * factor[:, :ff]).astype(BF).reshape(SIDE, SLOT, ff)
+        grad[q, :, :, pl.ds(ff, ff)] = (through * factor[:, ff:]).astype(BF).reshape(SIDE, SLOT, ff)
+        for i in range(SIDE):
+            source = q * SIDE + i
+            chosen = one_hot(table[source, pl.ds(me, 1), :]).astype(F32)
+            row = jnp.sum(chosen * comb[i * SLOT : (i + 1) * SLOT], axis=0, keepdims=True)
+            comb_out[source] = jnp.broadcast_to(row, comb_out.shape[1:])
+        if q + 2 < SIDE:
+            stream(q + 2)
+
+    comb_mid[pl.ds(y, 1)] = comb_out[pl.ds(pl.multiple_of(y * SIDE, SIDE), SIDE)][None]
+    comb_cols = [
+        remote(
+            comb_out.at[pl.ds(mod4(y + i) * SIDE, SIDE)], comb_mid.at[y],
+            comb_send.at[i - 1], comb_recv.at[i - 1], expert=col_peers[i - 1],
+        )
+        for i in (1, 2, 3)
+    ]
+    comb_rows = [
+        remote(
+            comb_mid.at[:, mod4(x + i)], comb_in.at[x],
+            comb_send.at[2 + i], comb_recv.at[2 + i], expert=row_peers[i - 1],
+        )
+        for i in (1, 2, 3)
+    ]
+    for copy in comb_cols:
+        go(copy)
+
+    def turn_comb():
+        for copy in comb_cols:
+            copy.wait_recv()
+        for copy in comb_rows:
+            go(copy)
+        comb_in[pl.ds(x, 1)] = comb_mid[:, pl.ds(x, 1)].reshape(1, SIDE, *comb_in.shape[2:])
+
+    def sem(c, half, i):
+        return send.at[c, half, i], recv.at[c, half, i]
+
+    def tile(half, c, j):
+        u, v = uv[half]
+        cols = pl.ds(*chunks[c])
+        vj = mod4(v + j)
+        if half == 0:
+            rows = grad[pl.ds(vj, 1)]
+        else:
+            rows = grad[:, pl.ds(vj, 1)]
+        out = contract(rows.reshape(group, 2 * ff), wgu[half, cols, :], 1, 1).astype(BF)
+        up, down = at(half, u, mod4(v + 1)), at(half, u, mod4(v + 3))
+        if j == 0:
+            returned[pl.ds(half, 1), :, pl.ds(v, 1), :, cols] = out.reshape(1, SIDE, 1, SLOT, -1)
+            return
+        outgoing[half, j - 1, :, :, cols] = out.reshape(SIDE, SLOT, -1)
+        piece = outgoing.at[half, j - 1]
+        if j == 2:
+            go(remote(piece.at[pl.ds(0, 2), :, cols], relayed.at[half, 0, :, :, cols], *sem(c, half, 0), expert=up))
+            go(remote(piece.at[pl.ds(2, 2), :, cols], relayed.at[half, 1, :, :, cols], *sem(c, half, 1), expert=down))
+        else:
+            go(remote(
+                piece.at[:, :, cols], returned.at[half, :, v, :, cols],
+                *sem(c, half, 2 + j // 2), expert=up if j == 1 else down,
+            ))
+
+    def forward(half, c):
+        u, v = uv[half]
+        cols = pl.ds(*chunks[c])
+        up, down = at(half, u, mod4(v + 1)), at(half, u, mod4(v + 3))
+        for d, to, origin in ((0, up, mod4(v + 3)), (1, down, mod4(v + 1))):
+            slot = relayed.at[half, d, :, :, cols]
+            remote(slot, slot, *sem(c, half, d), expert=to).wait_recv()
+            go(remote(slot, returned.at[half, pl.ds(2 * d, 2), origin, :, cols], *sem(c, half, 4 + d), expert=to))
+
+    def turn(half, c):
+        u, v = uv[half]
+        start, size = chunks[c]
+        cols = pl.ds(start, size)
+        up, down = at(half, mod4(u + 1), v), at(half, mod4(u + 3), v)
+        for d in (0, 1):
+            piece = returned.at[half, :, 0, :, cols]
+            remote(piece, piece, *sem(c, half, 2 + d), expert=up).wait_recv()
+            piece = returned.at[half, pl.ds(0, 2), 0, :, cols]
+            remote(piece, piece, *sem(c, half, 4 + d), expert=up).wait_recv()
+        for o in (2, 1, 3, 0):
+            uo = mod4(u + o)
+            source = at(half, uo, v)
+            maps = jnp.concatenate(
+                [one_hot(table[pl.ds(source, 1), pl.ds(at(half, u, w), 1), :][0]) for w in range(SIDE)],
+                axis=0,
+            )
+            rows = returned[pl.ds(half, 1), pl.ds(uo, 1), :, :, cols].reshape(group, size)
+            total = contract(maps, rows, 0, 0)
+            if o == 2:
+                sending[half, 0, :, cols] = total.astype(BF)
+                low, high = pl.ds(0, TOK // 2), pl.ds(TOK // 2, TOK // 2)
+                go(remote(sending.at[half, 0, low, cols], half_in.at[half, 0, :, cols], *sem(c, half, 6), expert=up))
+                go(remote(sending.at[half, 0, high, cols], half_in.at[half, 1, :, cols], *sem(c, half, 7), expert=down))
+            else:
+                partial[half, o // 2 if o else 2, :, pl.ds(0, size)] = total
+
+    def add_up(half, c):
+        u, v = uv[half]
+        start, size = chunks[c]
+        cols = pl.ds(start, size)
+        up, down = at(half, mod4(u + 1), v), at(half, mod4(u + 3), v)
+        for d, to in ((0, up), (1, down)):
+            piece = half_in.at[half, d, :, cols]
+            remote(piece, piece, *sem(c, half, 6 + d), expert=to).wait_recv()
+            met = pl.ds(d * (TOK // 2), TOK // 2)
+            other = pl.ds((1 - d) * (TOK // 2), TOK // 2)
+            sending[half, 1 + d, met, cols] = (
+                partial[half, d, met, pl.ds(0, size)] + half_in[half, d, :, cols].astype(F32)
+            ).astype(BF)
+            sending[half, 1 + d, other, cols] = partial[half, d, other, pl.ds(0, size)].astype(BF)
+            go(remote(sending.at[half, 1 + d, :, cols], full_in.at[half, d, :, cols], *sem(c, half, 8 + d), expert=to))
+
+    def finish(half, c):
+        start, size = chunks[c]
+        cols = pl.ds(start, size)
+        for d in (0, 1):
+            piece = full_in.at[half, d, :, cols]
+            remote(piece, piece, *sem(c, half, 8 + d), expert=me).wait_recv()
+        total = partial[half, 2, :, pl.ds(0, size)] + (
+            full_in[half, 0, :, cols].astype(F32) + full_in[half, 1, :, cols].astype(F32)
+        )
+        place = pl.ds(half * width + start, size)
+        final[:, place] = total.astype(BF)
+        go(remote(final.at[:, place], passed.at[:, place], *sem(c, half, 10), pipe=mod4(pipe + 3)))
+
+    busy = {}
+
+    def put(key, copy):
+        busy[key] = copy
+        copy.start()
+
+    def free(key):
+        if key in busy:
+            copy, away = busy.pop(key)
+            copy.wait_send() if away else copy.wait()
+
+    units = []
+    gu_step = 256
+    gu_count = width // gu_step
+    dn_cuts = DN_CUTS
+
+    def gate_up_unit(away, i):
+        side = 1 - dp if away else dp
+        n = (0 if away else gu_count) + i
+        key = ("gu", n % 2)
+        left = saved[pl.ds(side, 1), :, pl.ds(i * gu_step, gu_step)][0]
+        out = contract(left, grad[...].reshape(SIDE * group, 2 * ff), 0, 0).astype(BF)
+        free(key)
+        gu_stage[n % 2] = out
+        rows = pl.ds(i * gu_step, gu_step)
+        if away:
+            copy = remote(gu_stage.at[n % 2], gu_recv.at[rows], dw_send.at[i], dw_recv.at[i], dp=1 - dp)
+            arrivals.append(copy)
+        else:
+            copy = pltpu.make_async_copy(gu_stage.at[n % 2], gu_own.at[rows], own_sem.at[i])
+        copy.start()
+        busy[key] = (copy, away)
+
+    def down_unit(away, i):
+        side = 1 - dp if away else dp
+        n = (0 if away else len(dn_cuts)) + i
+        key = ("dn", n % 2)
+        rows = pl.ds(*dn_cuts[i])
+        slot = dn_stage.at[n % 2, pl.ds(0, dn_cuts[i][1])]
+        right = dy[pl.ds(side, 1)].reshape(SIDE * group, width)
+        out = contract(scaled[:, rows], right, 0, 0).astype(BF)
+        free(key)
+        slot[...] = out
+        if away:
+            copy = remote(slot, dn_recv.at[rows], dw_send.at[gu_count + i], dw_recv.at[gu_count + i], dp=1 - dp)
+            arrivals.append(copy)
+        else:
+            copy = pltpu.make_async_copy(slot, dn_own.at[rows], own_sem.at[gu_count + i])
+        copy.start()
+        busy[key] = (copy, away)
+
+    arrivals = []
+    for away in (True, False):
+        units += [functools.partial(down_unit, away, i) for i in range(len(dn_cuts))]
+        units += [functools.partial(gate_up_unit, away, i) for i in range(gu_count)]
+
+    def work(count):
+        for _ in range(min(count, len(units))):
+            units.pop(0)()
+
+    both = (0, 1)
+    loads["wgu_own"].wait()
+    loads["wgu_peer"].wait()
+    for j in (2, 1, 3, 0):
+        for half in both:
+            tile(half, 0, j)
+    for half in both:
+        forward(half, 0)
+    turn_comb()
+    for j in (2, 1, 3, 0):
+        for half in both:
+            tile(half, 1, j)
+    for name in ("scaled", "in0", "in1"):
+        loads[name].wait()
+    work(1)
+    for half in both:
+        forward(half, 1)
+    work(2)
+    for half in both:
+        turn(half, 0)
+    work(2)
+    for half in both:
+        add_up(half, 0)
+    work(3)
+    for half in both:
+        finish(half, 0)
+    work(3)
+    for half in both:
+        turn(half, 1)
+    work(2)
+    for half in both:
+        add_up(half, 1)
+    work(len(units))
+    for half in both:
+        finish(half, 1)
+    for key in list(busy):
+        free(key)
+    for copy in arrivals + comb_rows:
+        copy.wait_recv()
+    for c, (start, size) in enumerate(chunks):
+        for half in both:
+            place = pl.ds(half * width + start, size)
+            piece = passed.at[:, place]
+            remote(piece, piece, *sem(c, half, 10), pipe=mod4(pipe + 3)).wait_recv()
+    for copy in sends:
+        copy.wait_send()
+
+
+def backward(dya, dyb, table, wgu_own, wgu_peer, wdn_own, wdn_peer, coef, hidden, scaled, inputs):
+    width = dya.shape[-1]
+    rows, ff = hidden.shape
+    group = SIDE * SLOT
+    vmem = pl.BlockSpec(memory_space=pltpu.VMEM)
+    anyw = pl.BlockSpec(memory_space=pltpu.HBM)
+    widest = max(size for _, size in CHUNKS)
+    cut = max(size for _, size in DN_CUTS)
+    dma = pltpu.SemaphoreType.DMA
+    return pl.pallas_call(
+        backward_kernel,
+        out_shape=(
+            jax.ShapeDtypeStruct((TOK, 2 * width), BF),
+            jax.ShapeDtypeStruct((SIDE, SIDE, 8, TOK), F32),
+            jax.ShapeDtypeStruct(wgu_own.shape, BF),
+            jax.ShapeDtypeStruct(wgu_own.shape, BF),
+            jax.ShapeDtypeStruct(wdn_own.shape, BF),
+            jax.ShapeDtypeStruct(wdn_own.shape, BF),
+        ),
+        in_specs=[anyw, anyw, vmem] + [anyw] * 8,
+        out_specs=(anyw, vmem, anyw, anyw, anyw, anyw),
+        scratch_shapes=[
+            pltpu.VMEM((2,) + wgu_own.shape, BF),
+            pltpu.VMEM((2,) + wdn_own.shape, BF),
+            pltpu.VMEM((2, EXPERTS, SLOT, width), BF),
+            pltpu.VMEM((2, rows, width), BF),
+            pltpu.VMEM((rows, ff), BF),
+            pltpu.VMEM((2, group, 2 * ff), F32),
+            pltpu.VMEM((2, group, ff), F32),
+            pltpu.VMEM((SIDE, SIDE, SLOT, 2 * ff), BF),
+            pltpu.VMEM((2, 3, SIDE, SLOT, width), BF),
+            pltpu.VMEM((2, SIDE, SIDE, SLOT, width), BF),
+            pltpu.VMEM((2, 2, 2, SLOT, width), BF),
+            pltpu.VMEM((2, 3, TOK, widest), F32),
+            pltpu.VMEM((2, 3, TOK, width), BF),
+            pltpu.VMEM((2, 2, TOK // 2, width), BF),
+            pltpu.VMEM((2, 2, TOK, width), BF),
+            pltpu.VMEM((TOK, 2 * width), BF),
+            pltpu.VMEM((EXPERTS, 8, TOK), F32),
+            pltpu.VMEM((SIDE, SIDE, 8, TOK), F32),
+            pltpu.VMEM((2, 256, 2 * ff), BF),
+            pltpu.VMEM((2, cut, width), BF),
+            dma((9,)),
+            dma((SIDE, 2)),
+            dma((len(CHUNKS), 2, 11)),
+            dma((len(CHUNKS), 2, 11)),
+            dma((6,)),
+            dma((6,)),
+            dma((8,)),
+            dma((8,)),
+            dma((8,)),
+        ],
+        compiler_params=pltpu.CompilerParams(
+            collective_id=1, has_side_effects=True, vmem_limit_bytes=64 * 1024 * 1024
+        ),
+        name="backward",
+    )(dya, dyb, table, wgu_own, wgu_peer, wdn_own, wdn_peer, coef, hidden, scaled, inputs)
+
+
+def body(out_grad, routes, combine, gate_up_weight, down_weight, saved_inputs, saved_gate_up):
     rt, cb = routes[0].T, combine[0].T.astype(F32)
-    dya, dyb, table, wgu_peer, wdn_peer = dispatch(out_grad[0], rt, cb, gate_up_weight[0, 0], down_weight[0, 0])
-    first = dp == 0
     own_gu, own_dn = gate_up_weight[0, 0], down_weight[0, 0]
-    gate_up = jnp.concatenate([jnp.where(first, own_gu, wgu_peer), jnp.where(first, wgu_peer, own_gu)], axis=0)
-    down_proj = jnp.concatenate([jnp.where(first, own_dn, wdn_peer), jnp.where(first, wdn_peer, own_dn)], axis=1)
-    dy = jnp.concatenate([dya, dyb], axis=2).reshape(1024, -1)
-    ids = jnp.arange(SLOT, dtype=F32)
-    s_all, w_all = table[:, :EXPERTS], table[:, EXPERTS:]
-    s_me = lax.dynamic_index_in_dim(s_all, me, 1, keepdims=False)
-    w_me = lax.dynamic_index_in_dim(w_all, me, 1, keepdims=False)
-    weight_rows = jnp.sum(jnp.where(ids[None, :, None] == s_me[:, None, :], w_me[:, None, :], 0.0), axis=2).reshape(-1)
-    gu_rows = saved_gate_up[0, 0, 0]
-    ff = gu_rows.shape[1] // 2
-    gate_pre = gu_rows[:, :ff].astype(F32)
-    up_pre = gu_rows[:, ff:].astype(F32)
-    logistic = jax.nn.sigmoid(gate_pre)
-    activated = gate_pre * logistic
-    hidden = activated * up_pre
-    through = lax.dot_general(dy, down_proj, (((1,), (1,)), ((), ())), preferred_element_type=F32)
-    comb_part = jnp.sum(through * hidden, axis=1).astype(BF)
-    factor = weight_rows[:, None]
-    scaled = (factor * hidden).astype(BF)
-    grad_hidden = factor * through
-    grad_gate = grad_hidden * up_pre * logistic * (1.0 + gate_pre * (1.0 - logistic))
-    grad_up = grad_hidden * activated
-    grad_gu = jnp.concatenate([grad_gate, grad_up], axis=1).astype(BF)
-    input_grad = lax.dot_general(grad_gu, gate_up, (((1,), (1,)), ((), ())), preferred_element_type=F32).astype(BF)
-    back = lax.all_to_all(input_grad.reshape(1, 16, SLOT, -1), "expert", split_axis=1, concat_axis=1, tiled=True)
-    comb = lax.all_to_all(comb_part.reshape(1, 16, SLOT), "expert", split_axis=1, concat_axis=1, tiled=True)[0]
-    s_own = lax.dynamic_index_in_dim(s_all, me, 0, keepdims=False)
-    onehot = (ids[None, :, None] == s_own[:, None, :]).astype(BF).reshape(1024, TOK)
-    layer = lax.dot_general(onehot, back.reshape(1024, -1), (((0,), (0,)), ((), ())), preferred_element_type=F32).astype(BF)
-    passed = shifted(layer[None], "pipe", -1)
-    comb_et = jnp.sum(onehot.reshape(16, SLOT, TOK).astype(F32) * comb[:, :, None].astype(F32), axis=1)
-    comb_grad = jnp.sum(jnp.where(rt[:, None, :] == jnp.arange(16)[None, :, None], comb_et[None], 0.0), axis=1).T.astype(BF)[None]
-    part_gu = jnp.einsum("rd,rf->df", saved_inputs[0, 0, 0], grad_gu, preferred_element_type=F32).astype(BF)
-    part_dn = jnp.einsum("rf,rd->fd", scaled, dy, preferred_element_type=F32).astype(BF)
-    sum_gu = lax.psum_scatter(part_gu, "dp", scatter_dimension=0, tiled=True)
-    sum_dn = lax.psum_scatter(part_dn, "dp", scatter_dimension=1, tiled=True)
-    return passed, comb_grad, sum_gu[None, None], sum_dn[None, None]
+    dya, dyb, table, wgu_peer, wdn_peer, coef, hidden, scaled = dispatch(
+        out_grad[0], rt, cb, own_gu, own_dn, saved_gate_up[0, 0, 0]
+    )
+    passed, comb, gu_own, gu_recv, dn_own, dn_recv = backward(
+        dya, dyb, table, own_gu, wgu_peer, own_dn, wdn_peer, coef, hidden, scaled, saved_inputs[0, 0, 0]
+    )
+    by_expert = jnp.swapaxes(comb[:, :, 0, :], 0, 1).reshape(EXPERTS, TOK)
+    ids = jnp.arange(EXPERTS, dtype=jnp.int32)
+    comb_grad = jnp.sum(jnp.where(rt[:, None, :] == ids[None, :, None], by_expert[None], 0.0), axis=1)
+    sum_gu = (gu_own.astype(F32) + gu_recv.astype(F32)).astype(BF)
+    sum_dn = (dn_own.astype(F32) + dn_recv.astype(F32)).astype(BF)
+    return passed[None], comb_grad.T.astype(BF)[None], sum_gu[None, None], sum_dn[None, None]
 
 
 def solution(mesh):

time: 250 us -> 145 us (0.58)
  Pallas kernels: 49.4 us -> 128 us
  waiting for transfers between devices: 77 us -> 0 us
  matrix products: 49.4 us -> 0 us
  local copies, waits for them, and re-layouts: 25.8 us -> 3.12 us
  between operations: 14.2 us -> 0.66 us
  blocking collectives: 12.5 us -> 0 us
  starting transfers between devices: 8.02 us -> 0 us
    pallas_call x0 -> x1, Pallas kernels: none -> 77 us  [backward(): pl.pallas_call(backward_kernel, out_shape=(jax.ShapeDtypeStruct((TOK, 2 *...]
    all_to_all x1 -> x0, waiting for transfers between devices: 77 us -> none  [body(): lax.all_to_all(input_grad.reshape(1, 16, SLOT, -1), 'expert', split_axis=...]
    dot_general x5 -> x0, matrix products: 49.4 us -> none  [the longest x1 14.1 us: body(): lax.dot_general(grad_gu, gate_up, (((1,), (1,)), ((), ())), preferred_ele...]
    unnamed x28 -> x6, local copies, waits for them, and re-layouts: 25.6 us -> 2.12 us
    all_to_all x1 -> x0, blocking collectives: 12.5 us -> none  [body(): lax.all_to_all(comb_part.reshape(1, 16, SLOT), 'expert', split_axis=1, co...]
    broadcast_in_dim x0 -> x2, other arithmetic: none -> 10.2 us  [the longest x1 5.9 us: body(): sum_gu[None, None]]
    select_n x2 -> x0, other arithmetic: 8.81 us -> none  [the longest x1 8.51 us: body(): jnp.where(first, own_gu, wgu_peer)]
    all_to_all x1 -> x0, starting transfers between devices: 4.72 us -> none  [body(): lax.all_to_all(input_grad.reshape(1, 16, SLOT, -1), 'expert', split_axis=...]
  transfers between devices with their start and end apart: 4 -> 0, of which waited for: 1 -> 0; matrix products, arithmetic and copies ran while one was open for 18% -> 0% of each run, Pallas kernels for 0% -> 0%
where the time goes in v2:
time: 145 us
  Pallas kernels  128 us (88%)
  other arithmetic  13 us (9%)
  local copies, waits for them, and re-layouts  3.12 us (2%)
    pallas_call x1, Pallas kernels, backward(): pl.pallas_call(backward_kernel, out_shape=(jax.ShapeDtypeStruct((TOK, 2 *...  77 us
    pallas_call x1, Pallas kernels, dispatch(): pl.pallas_call(dispatch_kernel, out_shape=(block, block, jax.ShapeDtypeSt...  51.4 us
    broadcast_in_dim x1, other arithmetic, body(): sum_gu[None, None]  5.9 us
    broadcast_in_dim x1, other arithmetic, body(): sum_dn[None, None]  4.27 us

profile of v2, /device:TPU:0, one launch (start us, length us, event | category | flops | bytes accessed | tf_op | source)
XLA Modules:
  0.0 145.2 jit_solution(11550399889498490625)
XLA Ops:
  0.6 1.3 copy.15
  1.9 1.3 convert_bitcast_fusion.combine
  3.2 51.4 %dispatch.1 = (bf16[16,64,1280]{2,1,0:T(8,128)(2,1)}, bf16[16,64,1280]{2,1,0:T(8,128)(2,1)}, f32[16,32,128]{2,1,0:T(8,128)}, bf16[1280,1792]{1,0:T(8,128)(2,1)},...) custom-call(bf16[128,2560]{1,0:T(8,128)(2,1)} %bitcast.35, ...), custom_call_target="tpu_custom_call" | custom-call | tf_op jit(solution)/shard_map/dispatch/pallas_call | solution.py:251
  54.6 77.0 %backward.1 = (bf16[128,2560]{1,0:T(8,128)(2,1)}, f32[4,4,8,128]{3,2,1,0:T(8,128)}, bf16[1280,1792]{1,0:T(8,128)(2,1)}, bf16[1280,1792]{1,0:T(8,128)(2,1)}, bf16...) custom-call(bf16[16,64,1280]{2,1,0:T(8,128)(2,1)} %get-tuple-element.18.dya, ...), custom_call_target="tpu_custom_call" | custom-call | tf_op jit(solution)/shard_map/backward/pallas_call | solution.py:602
  131.7 0.0 copy-start
  131.7 1.0 slice.3
  132.7 1.5 %select_reduce_fusion = bf16[6,128]{1,0:T(8,128)(2,1)} fusion(f32[16,128]{1,0:T(8,128)S(1)} %bitcast.39, s32[6,128]{1,0:T(8,128)} %bitcast.38), kind=kLoop, calls=%fused_computation.4 | loop fusion | flops 36096 | bytes 12800 | tf_op jit(solution)/shard_map/reduce_sum | solution.py:663
  134.2 4.3 %fusion.1 = bf16[1,1,896,1280]{3,2,1,0:T(8,128)(2,1)} fusion(bf16[896,1280]{1,0:T(8,128)(2,1)} %get-tuple-element.31, bf16[896,1280]{1,0:T(8,128)(2,1)} %get-tuple-element.30), kind=kLoop, calls=%fused_computation.3 | loop fusion | flops 4587520 | bytes 6881280 | tf_op jit(solution)/shard_map/broadcast_in_dim | solution.py:666
  138.5 0.0 copy-done
  138.5 0.0 copy-start.1
  138.5 5.9 %fusion = bf16[1,1,1280,1792]{3,2,1,0:T(8,128)(2,1)} fusion(bf16[1280,1792]{1,0:T(8,128)(2,1)} %get-tuple-element.29, bf16[1280,1792]{1,0:T(8,128)(2,1)S(1)} %copy-done), kind=kLoop, calls=%fused_computation.1 | loop fusion | flops 9175040 | bytes 13762560 | tf_op jit(solution)/shard_map/broadcast_in_dim | solution.py:666
  144.4 0.0 copy-done.1
  144.4 0.8 copy.17
  (1 shorter events, 0.0 us)
Async XLA Ops:
  131.7 6.8 %copy-start = (bf16[1280,1792]{1,0:T(8,128)(2,1)S(1)}, bf16[1280,1792]{1,0:T(8,128)(2,1)}, u32[]{:S(2)}) copy-start(bf16[1280,1792]{1,0:T(8,128)(2,1)} %get-tuple-element.28) | copy-start | bytes 13762564
  138.5 5.9 %copy-start.1 = (bf16[128,2560]{1,0:T(8,128)(2,1)S(1)}, bf16[128,2560]{1,0:T(8,128)(2,1)}, u32[]{:S(2)}) copy-start(bf16[128,2560]{1,0:T(8,128)(2,1)} %get-tuple-element.26) | copy-start | bytes 1966084

commit v3 on v1

v3 whole, which is shorter than its diff:
```python
import functools

import jax
import jax.numpy as jnp
from jax import lax
from jax.experimental import pallas as pl
from jax.experimental.pallas import tpu as pltpu
from jax.sharding import PartitionSpec as P

SLOT = 64
SIDE = 4
TOK = 128
EXPERTS = 16
TOP = 6
MESH = pl.DeviceIdType.MESH
BF = jnp.bfloat16
F32 = jnp.float32
ORDER = (0, 1, 3, 2)
PLACE = (0, 1, 3, 2)
CHUNKS = ((0, 768), (768, 512))
GU_STEP = 256
DN_CUTS = ((0, 256), (256, 256), (512, 384))
BOTH = (0, 1)
PACE = (5, 2, 2, 3, 2, 2)
LOW, HIGH = pl.ds(0, TOK // 2), pl.ds(TOK // 2, TOK // 2)


def mod4(i):
    return lax.rem(i, SIDE)


def at(half, u, v):
    return v * SIDE + u if half == 0 else u * SIDE + v


def remote(src, dst, send, recv, **where):
    return pltpu.make_async_remote_copy(
        src_ref=src, dst_ref=dst, send_sem=send, recv_sem=recv, device_id=where, device_id_type=MESH
    )


def enter(**peers):
    barrier = pltpu.get_barrier_semaphore()
    count = 0
    for axis, indices in peers.items():
        for index in indices:
            pl.semaphore_signal(barrier, inc=1, device_id={axis: index}, device_id_type=MESH)
            count += 1
    pl.semaphore_wait(barrier, count)


def same_slot(slots_row):
    ids = lax.broadcasted_iota(jnp.int32, (SLOT, TOK), 0).astype(F32)
    return ids == slots_row


def one_hot(slots_row):
    return jnp.where(same_slot(slots_row), 1.0, 0.0).astype(BF)


def contract(a, b, da, db):
    return lax.dot_general(a, b, (((da,), (db,)), ((), ())), preferred_element_type=F32)


def layer_kernel(
    tok, picks, wgu_in, wdn_in, inputs_in, gate_up_in,
    passed, comb_grad, gu_grad, dn_grad, gu_part, dn_part,
    wgu, wdn, dy, saved, grad, scaled, table,
    gathered, staged, outgoing, returned, partial, sending, half_in, full_in, final,
    comb_out, comb_mid, comb_in, gu_stage, dn_stage, gu_other, dn_other,
    load_sem, held_sem, saved_sem, ring_send, ring_recv, slot_send, slot_recv, table_send, table_recv,
    dp_send, dp_recv, back_send, back_recv, comb_send, comb_recv, dw_send, dw_recv, own_sem, other_sem,
):
    me = lax.axis_index("expert")
    dp = lax.axis_index("dp")
    pipe = lax.axis_index("pipe")
    y, x = lax.div(me, SIDE), lax.rem(me, SIDE)
    width = dy.shape[-1]
    ff = scaled.shape[-1]
    group = SIDE * SLOT
    uv = ((x, y), (y, x))
    row_peers = [y * SIDE + mod4(x + i) for i in (1, 2, 3)]
    col_peers = [mod4(y + i) * SIDE + x for i in (1, 2, 3)]

    loads = {}

    def load(name, src, dst, sem):
        loads[name] = pltpu.make_async_copy(src, dst, sem)
        loads[name].start()

    def need(*names):
        for name in names:
            if name in loads:
                loads.pop(name).wait()

    def block_rows(i, k):
        source = mod4(y + ORDER[i]) * SIDE + mod4(x + ORDER[k])
        return source, pl.ds(pl.multiple_of(source * SLOT, SLOT), SLOT)

    enter(
        expert=row_peers + col_peers,
        dp=[1 - dp],
        pipe=[mod4(pipe + 1), mod4(pipe + 3)],
    )
    sends = []

    def go(copy):
        copy.start()
        sends.append(copy)
        return copy

    def ring(half, step):
        u, v = uv[half]
        up, down = at(half, mod4(u + 1), v), at(half, mod4(u + 3), v)
        if step == 0:
            mine = tok.at[:, pl.ds(half * width, width)]
            return (
                remote(mine, gathered.at[half, 0], ring_send.at[half, 0], ring_recv.at[half, 0], expert=down),
                remote(mine, gathered.at[half, 1], ring_send.at[half, 1], ring_recv.at[half, 1], expert=up),
            )
        return (
            remote(
                gathered.at[half, 0, LOW], gathered.at[half, 2, LOW],
                ring_send.at[half, 2], ring_recv.at[half, 2], expert=down,
            ),
            remote(
                gathered.at[half, 1, HIGH], gathered.at[half, 2, HIGH],
                ring_send.at[half, 3], ring_recv.at[half, 3], expert=up,
            ),
        )

    near = [ring(half, 0) for half in BOTH]
    for half in BOTH:
        for copy in near[half]:
            go(copy)

    ids = lax.broadcasted_iota(jnp.int32, (EXPERTS, TOK), 0).astype(F32)
    chosen = jnp.zeros((EXPERTS, TOK), F32)
    weight = jnp.zeros((EXPERTS, TOK), F32)
    for k in range(TOP):
        hit = jnp.where(ids == picks[pl.ds(k, 1), :], 1.0, 0.0)
        chosen = chosen + hit
        weight = weight + hit * picks[pl.ds(TOP + k, 1), :]
    before = lax.broadcasted_iota(jnp.int32, (TOK, TOK), 0) < lax.broadcasted_iota(
        jnp.int32, (TOK, TOK), 1
    )
    count = jnp.dot(
        chosen.astype(BF), jnp.where(before, 1.0, 0.0).astype(BF), preferred_element_type=F32
    )
    slots = jnp.where(chosen > 0.5, count, -1.0)
    table[pl.ds(me, 1)] = jnp.concatenate([slots, weight], axis=0)[None]

    row_tables = [
        remote(table.at[me], table.at[me], table_send.at[i], table_recv.at[i], expert=row_peers[i])
        for i in range(3)
    ]
    for copy in row_tables:
        go(copy)
    across = [
        remote(wdn_in, wdn.at[dp], dp_send.at[0], dp_recv.at[0], dp=1 - dp),
        remote(wgu_in, wgu.at[dp], dp_send.at[1], dp_recv.at[1], dp=1 - dp),
    ]
    for copy in across:
        go(copy)
    load("wdn", wdn_in, wdn.at[dp], load_sem.at[0])
    for i in range(SIDE):
        for k in range(SIDE):
            load(("held", i, k), gate_up_in.at[block_rows(i, k)[1]], grad.at[i, k], held_sem.at[i, k])
    load("wgu", wgu_in, wgu.at[dp], load_sem.at[1])
    for i in range(SIDE):
        for k in range(SIDE):
            load(("saved", i, k), inputs_in.at[block_rows(i, k)[1]], saved.at[i, k], saved_sem.at[i, k])

    def slots_of(source, expert):
        return table[pl.ds(source, 1), pl.ds(expert, 1), :][0]

    arrivals = {}

    def arrived(half, r, j):
        if (half, r, j) in arrivals:
            arrivals.pop((half, r, j)).wait_recv()

    def deliver(half, r):
        u, v = uv[half]
        source = at(half, mod4(u + ORDER[r]), v)
        maps = [one_hot(slots_of(source, at(half, u, mod4(v + j)))) for j in (2, 1, 3, 0)]
        if r == 0:
            block = tok[:, pl.ds(half * width, width)]
        else:
            block = gathered[half, r - 1]
        rows = jnp.dot(jnp.concatenate(maps, axis=0), block, preferred_element_type=F32)
        rows = rows.astype(BF).reshape(SIDE, SLOT, width)
        for n, j in enumerate((2, 1, 3, 0)):
            there = PLACE[(SIDE - j) % SIDE]
            i, k = (there, r) if half == 0 else (r, there)
            if j == 0:
                dy[half, i, k] = rows[n]
            else:
                staged[half, j - 1, r] = rows[n]
                copy = remote(
                    staged.at[half, j - 1, r], dy.at[half, i, k],
                    slot_send.at[half, r, j - 1], slot_recv.at[half, r, j - 1],
                    expert=at(half, u, mod4(v + j)),
                )
                go(copy)
                arrivals[(half, r, j)] = copy

    def through_rows(blocks):
        need("wdn", "wdn_peer", *[("held", i, k) for i, k in blocks])
        for i, k in blocks:
            arrived(0, k, (SIDE - ORDER[i]) % SIDE)
            arrived(1, i, (SIDE - ORDER[k]) % SIDE)
        through = contract(jnp.concatenate([dy[0, i, k] for i, k in blocks], axis=0), wdn[0], 1, 1)
        through = through + contract(
            jnp.concatenate([dy[1, i, k] for i, k in blocks], axis=0), wdn[1], 1, 1
        )
        for n, (i, k) in enumerate(blocks):
            source = block_rows(i, k)[0]
            part = through[n * SLOT : (n + 1) * SLOT]
            same = same_slot(slots_of(source, me))
            given = table[pl.ds(source, 1), pl.ds(EXPERTS + me, 1), :][0]
            factor = jnp.sum(jnp.where(same, given, 0.0), axis=1, keepdims=True)
            gate = grad[i, k, :, pl.ds(0, ff)].astype(F32)
            up = grad[i, k, :, pl.ds(ff, ff)].astype(F32)
            logistic = 1.0 / (1.0 + jnp.exp(-gate))
            active = gate * logistic
            hidden = active * up
            comb = jnp.sum(part * hidden, axis=1, keepdims=True).astype(BF).astype(F32)
            row = jnp.sum(jnp.where(same, comb, 0.0), axis=0, keepdims=True)
            comb_out[i, k] = jnp.broadcast_to(row, comb_out.shape[2:])
            scaled[i, k] = (factor * hidden).astype(BF)
            weighted = factor * part
            slope = up * logistic * (1.0 + gate * (1.0 - logistic))
            grad[i, k, :, pl.ds(0, ff)] = (weighted * slope).astype(BF)
            grad[i, k, :, pl.ds(ff, ff)] = (weighted * active).astype(BF)

    def sem(c, half, i):
        return back_send.at[c, half, i], back_recv.at[c, half, i]

    waits = {}

    def tiles(half, c, pieces):
        u, v = uv[half]
        cols = pl.ds(*CHUNKS[c])
        rows = []
        for j, first, last, _ in pieces:
            for k in range(first, last):
                rows.append(grad[PLACE[j], k] if half == 0 else grad[k, PLACE[j]])
        out = contract(jnp.concatenate(rows, axis=0), wgu[half, cols, :], 1, 1).astype(BF)
        n = 0
        for j, first, last, number in pieces:
            span = last - first
            part = out[n * SLOT : (n + span) * SLOT].reshape(span, SLOT, -1)
            n += span
            if j == 0:
                returned[half, pl.ds(first, span), 0, :, cols] = part
                continue
            outgoing[half, j - 1, pl.ds(first, span), :, cols] = part
            copy = remote(
                outgoing.at[half, j - 1, pl.ds(first, span), :, cols],
                returned.at[half, pl.ds(first, span), PLACE[SIDE - j], :, cols],
                *sem(c, half, number),
                expert=at(half, u, mod4(v + j)),
            )
            go(copy)
            waits.setdefault((half, c), []).append(copy)

    def turn(half, c):
        u, v = uv[half]
        start, size = CHUNKS[c]
        cols = pl.ds(start, size)
        up, down = at(half, mod4(u + 1), v), at(half, mod4(u + 3), v)
        for copy in waits[(half, c)]:
            copy.wait_recv()
        for o in (2, 1, 3, 0):
            source = at(half, mod4(u + o), v)
            maps = jnp.concatenate(
                [one_hot(slots_of(source, at(half, u, mod4(v + w)))) for w in ORDER], axis=0
            )
            total = contract(maps, returned[half, PLACE[o], :, :, cols].reshape(group, size), 0, 0)
            if o == 2:
                sending[half, 0, :, cols] = total.astype(BF)
                go(remote(sending.at[half, 0, LOW, cols], half_in.at[half, 0, :, cols], *sem(c, half, 5), expert=up))
                go(remote(sending.at[half, 0, HIGH, cols], half_in.at[half, 1, :, cols], *sem(c, half, 6), expert=down))
            else:
                partial[half, (2, 0, 2, 1)[o], :, pl.ds(0, size)] = total

    def add_up(half, c):
        u, v = uv[half]
        start, size = CHUNKS[c]
        cols = pl.ds(start, size)
        up, down = at(half, mod4(u + 1), v), at(half, mod4(u + 3), v)
        for d, to, met, other in ((0, up, LOW, HIGH), (1, down, HIGH, LOW)):
            piece = half_in.at[half, d, :, cols]
            remote(piece, piece, *sem(c, half, 5 + d), expert=to).wait_recv()
            sending[half, 1 + d, met, cols] = (
                partial[half, d, met, pl.ds(0, size)] + half_in[half, d, :, cols].astype(F32)
            ).astype(BF)
            sending[half, 1 + d, other, cols] = partial[half, d, other, pl.ds(0, size)].astype(BF)
            go(remote(sending.at[half, 1 + d, :, cols], full_in.at[half, d, :, cols], *sem(c, half, 7 + d), expert=to))

    def finish(half, c):
        u, v = uv[half]
        start, size = CHUNKS[c]
        cols = pl.ds(start, size)
        for d, to in ((0, at(half, mod4(u + 1), v)), (1, at(half, mod4(u + 3), v))):
            piece = full_in.at[half, d, :, cols]
            remote(piece, piece, *sem(c, half, 7 + d), expert=to).wait_recv()
        total = partial[half, 2, :, pl.ds(0, size)] + (
            full_in[half, 0, :, cols].astype(F32) + full_in[half, 1, :, cols].astype(F32)
        )
        place = pl.ds(half * width + start, size)
        final[:, place] = total.astype(BF)
        go(remote(final.at[:, place], passed.at[:, place], *sem(c, half, 9), pipe=mod4(pipe + 3)))

    gu_count = width // GU_STEP
    busy = {}
    others = {}

    def free(key):
        if key in busy:
            copy, away = busy.pop(key)
            copy.wait_send() if away else copy.wait()

    def fetch(kind, i):
        n = i if kind == "gu" else gu_count + i
        ref, other = (gu_part, gu_other) if kind == "gu" else (dn_part, dn_other)
        rows = pl.ds(i * GU_STEP, GU_STEP) if kind == "gu" else pl.ds(*DN_CUTS[i])
        piece = ref.at[rows]
        remote(piece, piece, dw_send.at[n], dw_recv.at[n], dp=1 - dp).wait_recv()
        copy = pltpu.make_async_copy(piece, other.at[pl.ds(0, rows.size)], other_sem.at[n])
        copy.start()
        others[(kind, i)] = copy

    def grad_unit(kind, away, i):
        side = 1 - dp if away else dp
        if kind == "gu":
            count, n, rows = gu_count, i, pl.ds(i * GU_STEP, GU_STEP)
            cols = pl.ds(pl.multiple_of(side * width + i * GU_STEP, GU_STEP), GU_STEP)
            left = saved[:, :, :, cols].reshape(SIDE * group, GU_STEP)
            right = grad[...].reshape(SIDE * group, 2 * ff)
            stage, part, own, other = gu_stage, gu_part, gu_grad, gu_other
        else:
            count, n, rows = len(DN_CUTS), gu_count + i, pl.ds(*DN_CUTS[i])
            left = scaled[:, :, :, rows].reshape(SIDE * group, rows.size)
            right = dy[pl.ds(side, 1)].reshape(SIDE * group, width)
            stage, part, own, other = dn_stage, dn_part, dn_grad, dn_other
        turn_no = (0 if away else count) + i
        key = (kind, turn_no % 2)
        out = contract(left, right, 0, 0)
        free(key)
        slot = stage.at[turn_no % 2, pl.ds(0, rows.size)]
        if away:
            slot[...] = out.astype(BF)
            copy = remote(slot, part.at[rows], dw_send.at[n], dw_recv.at[n], dp=1 - dp)
        else:
            others.pop((kind, i)).wait()
            slot[...] = (out + other[pl.ds(0, rows.size), :].astype(F32)).astype(BF)
            if i + 1 < count:
                fetch(kind, i + 1)
            copy = pltpu.make_async_copy(slot, own.at[rows], own_sem.at[n])
        copy.start()
        busy[key] = (copy, away)

    units = [functools.partial(grad_unit, "dn", True, i) for i in range(len(DN_CUTS))]
    units += [functools.partial(grad_unit, "gu", True, i) for i in range(gu_count)]
    units += [functools.partial(fetch, "dn", 0), functools.partial(fetch, "gu", 0)]
    units += [functools.partial(grad_unit, "dn", False, i) for i in range(len(DN_CUTS))]
    units += [functools.partial(grad_unit, "gu", False, i) for i in range(gu_count)]

    def work(count):
        for _ in range(min(count, len(units))):
            units.pop(0)()

    for half in BOTH:
        deliver(half, 0)
    for copy in row_tables:
        copy.wait_recv()
    mine = pl.ds(y * SIDE, SIDE)
    col_tables = [
        remote(table.at[mine], table.at[mine], table_send.at[3 + i], table_recv.at[3 + i], expert=col_peers[i])
        for i in range(3)
    ]
    for copy in col_tables:
        go(copy)
    for half in BOTH:
        for copy in near[half]:
            copy.wait_recv()
        for copy in ring(half, 1):
            go(copy)
    for copy in col_tables:
        copy.wait_recv()
    for r in (1, 2):
        for half in BOTH:
            deliver(half, r)
    for half in BOTH:
        for copy in ring(half, 1):
            copy.wait_recv()
        deliver(half, 3)
    across[0].wait_recv()
    through_rows([(0, 0)])
    through_rows([(0, 1), (1, 0), (1, 1)])
    through_rows([(0, 2), (2, 0), (1, 2), (2, 1), (2, 2)])
    across[1].wait_recv()
    need("wgu")
    for c in BOTH:
        for half in BOTH:
            tiles(half, c, ((1, 0, 3, 0), (3, 0, 3, 1), (0, 0, 3, None)))
    through_rows([(0, 3), (3, 0), (1, 3), (3, 1)])
    through_rows([(2, 3), (3, 2), (3, 3)])
    comb_cols = [
        remote(
            comb_out.at[PLACE[i]], comb_mid.at[PLACE[SIDE - i]],
            comb_send.at[i - 1], comb_recv.at[i - 1], expert=col_peers[i - 1],
        )
        for i in (1, 2, 3)
    ]
    comb_rows = [
        remote(
            comb_mid.at[:, PLACE[i]], comb_in.at[PLACE[SIDE - i]],
            comb_send.at[2 + i], comb_recv.at[2 + i], expert=row_peers[i - 1],
        )
        for i in (1, 2, 3)
    ]
    comb_mid[0] = comb_out[0]
    for copy in comb_cols:
        go(copy)
    for c in BOTH:
        for half in BOTH:
            tiles(half, c, ((2, 0, 4, 2), (1, 3, 4, 3), (3, 3, 4, 4), (0, 3, 4, None)))
    for copy in comb_cols:
        copy.wait_recv()
    for copy in comb_rows:
        go(copy)
    comb_in[0] = comb_mid[:, 0]
    need(*[("saved", i, k) for i in range(SIDE) for k in range(SIDE)])
    work(PACE[0])
    for half in BOTH:
        turn(half, 0)
    work(PACE[1])
    for half in BOTH:
        add_up(half, 0)
    work(PACE[2])
    for half in BOTH:
        finish(half, 0)
    work(PACE[3])
    for half in BOTH:
        turn(half, 1)
    work(PACE[4])
    for half in BOTH:
        add_up(half, 1)
    work(PACE[5])
    for half in BOTH:
        finish(half, 1)
    work(len(units))
    for copy in comb_rows:
        copy.wait_recv()
    for k in range(TOP):
        total = jnp.zeros((1, TOK), F32)
        for i in range(SIDE):
            for j in range(SIDE):
                expert = mod4(y + ORDER[i]) * SIDE + mod4(x + ORDER[j])
                hit = picks[pl.ds(k, 1), :] == expert.astype(F32)
                total = total + jnp.where(hit, comb_in[j, i, pl.ds(0, 1), :], 0.0)
        comb_grad[pl.ds(k, 1), :] = total
    for key in list(busy):
        free(key)
    for c, (start, size) in enumerate(CHUNKS):
        for half in BOTH:
            place = pl.ds(half * width + start, size)
            piece = passed.at[:, place]
            remote(piece, piece, *sem(c, half, 9), pipe=mod4(pipe + 3)).wait_recv()
    for copy in sends:
        copy.wait_send()


def layer(tok, picks, wgu, wdn, inputs, gate_up):
    width, both = wgu.shape
    ff = both // 2
    vmem = pl.BlockSpec(memory_space=pltpu.VMEM)
    hbm = pl.BlockSpec(memory_space=pltpu.HBM)
    widest = max(size for _, size in CHUNKS)
    cut = max(size for _, size in DN_CUTS)
    count = width // GU_STEP + len(DN_CUTS)
    dma = pltpu.SemaphoreType.DMA
    return pl.pallas_call(
        layer_kernel,
        out_shape=(
            jax.ShapeDtypeStruct((TOK, 2 * width), BF),
            jax.ShapeDtypeStruct((TOP, TOK), F32),
            jax.ShapeDtypeStruct(wgu.shape, BF),
            jax.ShapeDtypeStruct(wdn.shape, BF),
            jax.ShapeDtypeStruct(wgu.shape, BF),
            jax.ShapeDtypeStruct(wdn.shape, BF),
        ),
        in_specs=[vmem, vmem, hbm, hbm, hbm, hbm],
        out_specs=(hbm, vmem, hbm, hbm, hbm, hbm),
        scratch_shapes=[
            pltpu.VMEM((2,) + wgu.shape, BF),
            pltpu.VMEM((2,) + wdn.shape, BF),
            pltpu.VMEM((2, SIDE, SIDE, SLOT, width), BF),
            pltpu.VMEM((SIDE, SIDE, SLOT, 2 * width), BF),
            pltpu.VMEM((SIDE, SIDE, SLOT, both), BF),
            pltpu.VMEM((SIDE, SIDE, SLOT, ff), BF),
            pltpu.VMEM((EXPERTS, 2 * EXPERTS, TOK), F32),
            pltpu.VMEM((2, 3, TOK, width), BF),
            pltpu.VMEM((2, 3, SIDE, SLOT, width), BF),
            pltpu.VMEM((2, 3, SIDE, SLOT, width), BF),
            pltpu.VMEM((2, SIDE, SIDE, SLOT, width), BF),
            pltpu.VMEM((2, 3, TOK, widest), F32),
            pltpu.VMEM((2, 3, TOK, width), BF),
            pltpu.VMEM((2, 2, TOK // 2, width), BF),
            pltpu.VMEM((2, 2, TOK, width), BF),
            pltpu.VMEM((TOK, 2 * width), BF),
            pltpu.VMEM((SIDE, SIDE, 8, TOK), F32),
            pltpu.VMEM((SIDE, SIDE, 8, TOK), F32),
            pltpu.VMEM((SIDE, SIDE, 8, TOK), F32),
            pltpu.VMEM((2, GU_STEP, both), BF),
            pltpu.VMEM((2, cut, width), BF),
            pltpu.VMEM((GU_STEP, both), BF),
            pltpu.VMEM((cut, width), BF),
            dma((2,)),
            dma((SIDE, SIDE)),
            dma((SIDE, SIDE)),
            dma((2, 4)),
            dma((2, 4)),
            dma((2, SIDE, 3)),
            dma((2, SIDE, 3)),
            dma((6,)),
            dma((6,)),
            dma((2,)),
            dma((2,)),
            dma((len(CHUNKS), 2, 10)),
            dma((len(CHUNKS), 2, 10)),
            dma((6,)),
            dma((6,)),
            dma((count,)),
            dma((count,)),
            dma((count,)),
            dma((count,)),
        ],
        compiler_params=pltpu.CompilerParams(
            collective_id=0, has_side_effects=True, vmem_limit_bytes=64 * 1024 * 1024
        ),
        name="layer",
    )(tok, picks, wgu, wdn, inputs, gate_up)


def body(out_grad, routes, combine, gate_up_weight, down_weight, saved_inputs, saved_gate_up):
    picks = jnp.concatenate([routes[0].T.astype(F32), combine[0].T.astype(F32)], axis=0)
    passed, comb, gu_grad, dn_grad, _, _ = layer(
        out_grad[0], picks, gate_up_weight[0, 0], down_weight[0, 0], saved_inputs[0, 0, 0], saved_gate_up[0, 0, 0]
    )
    return passed[None], comb.T.astype(BF)[None], gu_grad[None, None], dn_grad[None, None]


def solution(mesh):
    placed = (
        P("pipe", ("dp", "expert"), None),
        P("pipe", ("dp", "expert"), None),
        P("pipe", ("dp", "expert"), None),
        P("pipe", "expert", "dp", None),
        P("pipe", "expert", None, "dp"),
        P("pipe", "dp", "expert", None, None),
        P("pipe", "dp", "expert", None, None),
    )
    return jax.shard_map(
        body,
        mesh=mesh,
        in_specs=placed,
        out_specs=(
            P("pipe", ("dp", "expert"), None),
            P("pipe", ("dp", "expert"), None),
            P("pipe", "expert", "dp", None),
            P("pipe", "expert", None, "dp"),
        ),
        check_vma=False,
    )
```

time: 250 us -> 127 us (0.51)
  waiting for transfers between devices: 77 us -> 0 us
  Pallas kernels: 49.4 us -> 114 us
  matrix products: 49.4 us -> 0 us
  local copies, waits for them, and re-layouts: 25.8 us -> 8.24 us
  between operations: 14.2 us -> 0.64 us
  blocking collectives: 12.5 us -> 0 us
  other arithmetic: 13 us -> 3.23 us
  starting transfers between devices: 8.02 us -> 0 us
    all_to_all x1 -> x0, waiting for transfers between devices: 77 us -> none  [body(): lax.all_to_all(input_grad.reshape(1, 16, SLOT, -1), 'expert', split_axis=...]
    pallas_call x1, Pallas kernels: 49.4 us -> 114 us  [layer(): pl.pallas_call(layer_kernel, out_shape=(jax.ShapeDtypeStruct((TOK, 2 * wi...]
    dot_general x5 -> x0, matrix products: 49.4 us -> none  [the longest x1 14.1 us: body(): lax.dot_general(grad_gu, gate_up, (((1,), (1,)), ((), ())), preferred_ele...]
    unnamed x28 -> x5, local copies, waits for them, and re-layouts: 25.6 us -> 8.24 us
    all_to_all x1 -> x0, blocking collectives: 12.5 us -> none  [body(): lax.all_to_all(comb_part.reshape(1, 16, SLOT), 'expert', split_axis=1, co...]
    select_n x2 -> x0, other arithmetic: 8.81 us -> none  [the longest x1 8.51 us: body(): jnp.where(first, own_gu, wgu_peer)]
    all_to_all x1 -> x0, starting transfers between devices: 4.72 us -> none  [body(): lax.all_to_all(input_grad.reshape(1, 16, SLOT, -1), 'expert', split_axis=...]
    ppermute x1 -> x0, starting transfers between devices: 3.04 us -> none  [shifted(): return lax.ppermute(block, axis, route)]
  transfers between devices with their start and end apart: 4 -> 0, of which waited for: 1 -> 0; matrix products, arithmetic and copies ran while one was open for 18% -> 0% of each run, Pallas kernels for 0% -> 0%
where the time goes in v3:
time: 127 us; the launch traced here: 126 us
  Pallas kernels  114 us (90%)
  local copies, waits for them, and re-layouts  8.24 us (6%)
  other arithmetic  3.23 us (3%)
    pallas_call x1, Pallas kernels, layer(): pl.pallas_call(layer_kernel, out_shape=(jax.ShapeDtypeStruct((TOK, 2 * wi...  114 us
    unnamed x5, local copies, waits for them, and re-layouts  8.24 us

profile of v3, /device:TPU:0, one launch (start us, length us, event | category | flops | bytes accessed | tf_op | source)
XLA Modules:
  0.0 126.4 jit_solution(17041492959571737180)
XLA Ops:
  0.6 0.7 fusion
  1.3 0.7 convert_bitcast_fusion
  2.0 0.6 pad_maximum_fusion.picks
  2.6 114.3 %layer.1 = (bf16[128,2560]{1,0:T(8,128)(2,1)}, f32[6,128]{1,0:T(8,128)}, bf16[1280,1792]{1,0:T(8,128)(2,1)}, bf16[896,1280]{1,0:T(8,128)(2,1)}, bf16[1280,1792]{1,0:T(8,128)(2,1)}, /*index=5*/bf16[896,1280]{1,0:T(8,128)(2,1)}) custom-call(bf16[128,2560]{1,0:T(8,128)(2,1)} %bitcast.27, f32[12,128]{1,0:T(8,128)} %pad_maximum_fusion.picks, ...), custom_call_target="tpu_custom_call" | custom-call | tf_op jit(solution)/shard_map/layer/pallas_call | solution.py:486
  116.9 1.3 convert_bitcast_fusion.1
  118.2 2.0 %copy.18 = bf16[1,128,2560]{2,1,0:T(8,128)(2,1)} copy(bf16[1,128,2560]{2,1,0:T(8,128)(2,1)} %bitcast.28) | data formatting | bytes 1310720
  120.1 0.0 copy-start
  120.1 4.9 %copy.19 = bf16[1,1,1280,1792]{3,2,1,0:T(8,128)(2,1)} copy(bf16[1,1,1280,1792]{3,2,1,0:T(8,128)(2,1)} %bitcast.23) | data formatting | bytes 9175040
  125.0 0.0 copy-done
  125.0 1.4 %copy.20 = bf16[1,1,896,1280]{3,2,1,0:T(8,128)(2,1)} copy(bf16[1,1,896,1280]{3,2,1,0:T(8,128)(2,1)S(1)} %bitcast.26) | data formatting | bytes 4587520
Async XLA Ops:
  120.1 4.9 %copy-start = (bf16[896,1280]{1,0:T(8,128)(2,1)S(1)}, bf16[896,1280]{1,0:T(8,128)(2,1)}, u32[]{:S(2)}) copy-start(bf16[896,1280]{1,0:T(8,128)(2,1)} %get-tuple-element.11) | copy-start | bytes 6881284

commit v4 on v3

--- a/solution.py
+++ b/solution.py
@@ -17,11 +17,15 @@
 F32 = jnp.float32
 ORDER = (0, 1, 3, 2)
 PLACE = (0, 1, 3, 2)
-CHUNKS = ((0, 768), (768, 512))
+CHUNKS = ((0, 512), (512, 512), (1024, 256))
 GU_STEP = 256
 DN_CUTS = ((0, 256), (256, 256), (512, 384))
 BOTH = (0, 1)
-PACE = (5, 2, 2, 3, 2, 2)
+STEPS = (
+    (7, "turn", 0), (1, "add", 0), (2, "turn", 1), (1, "finish", 0), (1, "add", 1),
+    (2, "turn", 2), (1, "finish", 1), (1, "add", 2), (1, "finish", 2),
+)
+KEEP = (2, 10, 7)
 LOW, HIGH = pl.ds(0, TOK // 2), pl.ds(TOK // 2, TOK // 2)
 
 
@@ -39,14 +43,13 @@
     )
 
 
-def enter(**peers):
-    barrier = pltpu.get_barrier_semaphore()
+def greet(barrier, **peers):
     count = 0
     for axis, indices in peers.items():
         for index in indices:
             pl.semaphore_signal(barrier, inc=1, device_id={axis: index}, device_id_type=MESH)
             count += 1
-    pl.semaphore_wait(barrier, count)
+    return count
 
 
 def same_slot(slots_row):
@@ -97,7 +100,9 @@
         source = mod4(y + ORDER[i]) * SIDE + mod4(x + ORDER[k])
         return source, pl.ds(pl.multiple_of(source * SLOT, SLOT), SLOT)
 
-    enter(
+    barrier = pltpu.get_barrier_semaphore()
+    greeted = greet(
+        barrier,
         expert=row_peers + col_peers,
         dp=[1 - dp],
         pipe=[mod4(pipe + 1), mod4(pipe + 3)],
@@ -129,10 +134,14 @@
             ),
         )
 
-    near = [ring(half, 0) for half in BOTH]
-    for half in BOTH:
-        for copy in near[half]:
-            go(copy)
+    load("wdn", wdn_in, wdn.at[dp], load_sem.at[0])
+    for i in range(SIDE):
+        for k in range(SIDE):
+            load(("held", i, k), gate_up_in.at[block_rows(i, k)[1]], grad.at[i, k], held_sem.at[i, k])
+    load("wgu", wgu_in, wgu.at[dp], load_sem.at[1])
+    for i in range(SIDE):
+        for k in range(SIDE):
+            load(("saved", i, k), inputs_in.at[block_rows(i, k)[1]], saved.at[i, k], saved_sem.at[i, k])
 
     ids = lax.broadcasted_iota(jnp.int32, (EXPERTS, TOK), 0).astype(F32)
     chosen = jnp.zeros((EXPERTS, TOK), F32)
@@ -150,6 +159,12 @@
     slots = jnp.where(chosen > 0.5, count, -1.0)
     table[pl.ds(me, 1)] = jnp.concatenate([slots, weight], axis=0)[None]
 
+    pl.semaphore_wait(barrier, greeted)
+    near = [ring(half, 0) for half in BOTH]
+    for half in BOTH:
+        for copy in near[half]:
+            go(copy)
+
     row_tables = [
         remote(table.at[me], table.at[me], table_send.at[i], table_recv.at[i], expert=row_peers[i])
         for i in range(3)
@@ -162,15 +177,6 @@
     ]
     for copy in across:
         go(copy)
-    load("wdn", wdn_in, wdn.at[dp], load_sem.at[0])
-    for i in range(SIDE):
-        for k in range(SIDE):
-            load(("held", i, k), gate_up_in.at[block_rows(i, k)[1]], grad.at[i, k], held_sem.at[i, k])
-    load("wgu", wgu_in, wgu.at[dp], load_sem.at[1])
-    for i in range(SIDE):
-        for k in range(SIDE):
-            load(("saved", i, k), inputs_in.at[block_rows(i, k)[1]], saved.at[i, k], saved_sem.at[i, k])
-
     def slots_of(source, expert):
         return table[pl.ds(source, 1), pl.ds(expert, 1), :][0]
 
@@ -283,7 +289,7 @@
                 go(remote(sending.at[half, 0, LOW, cols], half_in.at[half, 0, :, cols], *sem(c, half, 5), expert=up))
                 go(remote(sending.at[half, 0, HIGH, cols], half_in.at[half, 1, :, cols], *sem(c, half, 6), expert=down))
             else:
-                partial[half, (2, 0, 2, 1)[o], :, pl.ds(0, size)] = total
+                partial[half, (2 + c % 2, 0, 2, 1)[o], :, pl.ds(0, size)] = total
 
     def add_up(half, c):
         u, v = uv[half]
@@ -306,7 +312,7 @@
         for d, to in ((0, at(half, mod4(u + 1), v)), (1, at(half, mod4(u + 3), v))):
             piece = full_in.at[half, d, :, cols]
             remote(piece, piece, *sem(c, half, 7 + d), expert=to).wait_recv()
-        total = partial[half, 2, :, pl.ds(0, size)] + (
+        total = partial[half, 2 + c % 2, :, pl.ds(0, size)] + (
             full_in[half, 0, :, cols].astype(F32) + full_in[half, 1, :, cols].astype(F32)
         )
         place = pl.ds(half * width + start, size)
@@ -403,7 +409,7 @@
     through_rows([(0, 2), (2, 0), (1, 2), (2, 1), (2, 2)])
     across[1].wait_recv()
     need("wgu")
-    for c in BOTH:
+    for c in range(len(CHUNKS)):
         for half in BOTH:
             tiles(half, c, ((1, 0, 3, 0), (3, 0, 3, 1), (0, 0, 3, None)))
     through_rows([(0, 3), (3, 0), (1, 3), (3, 1)])
@@ -425,7 +431,7 @@
     comb_mid[0] = comb_out[0]
     for copy in comb_cols:
         go(copy)
-    for c in BOTH:
+    for c in range(len(CHUNKS)):
         for half in BOTH:
             tiles(half, c, ((2, 0, 4, 2), (1, 3, 4, 3), (3, 3, 4, 4), (0, 3, 4, None)))
     for copy in comb_cols:
@@ -434,24 +440,11 @@
         go(copy)
     comb_in[0] = comb_mid[:, 0]
     need(*[("saved", i, k) for i in range(SIDE) for k in range(SIDE)])
-    work(PACE[0])
-    for half in BOTH:
-        turn(half, 0)
-    work(PACE[1])
-    for half in BOTH:
-        add_up(half, 0)
-    work(PACE[2])
-    for half in BOTH:
-        finish(half, 0)
-    work(PACE[3])
-    for half in BOTH:
-        turn(half, 1)
-    work(PACE[4])
-    for half in BOTH:
-        add_up(half, 1)
-    work(PACE[5])
-    for half in BOTH:
-        finish(half, 1)
+    steps = {"turn": turn, "add": add_up, "finish": finish}
+    for count, step, c in STEPS:
+        work(count)
+        for half in BOTH:
+            steps[step](half, c)
     work(len(units))
     for copy in comb_rows:
         copy.wait_recv()
@@ -507,7 +500,7 @@
             pltpu.VMEM((2, 3, SIDE, SLOT, width), BF),
             pltpu.VMEM((2, 3, SIDE, SLOT, width), BF),
             pltpu.VMEM((2, SIDE, SIDE, SLOT, width), BF),
-            pltpu.VMEM((2, 3, TOK, widest), F32),
+            pltpu.VMEM((2, 4, TOK, widest), F32),
             pltpu.VMEM((2, 3, TOK, width), BF),
             pltpu.VMEM((2, 2, TOK // 2, width), BF),
             pltpu.VMEM((2, 2, TOK, width), BF),
@@ -546,11 +539,53 @@
     )(tok, picks, wgu, wdn, inputs, gate_up)
 
 
+def keep_kernel(*refs):
+    n = len(KEEP)
+    sources, kept, held = refs[:n], refs[n : 2 * n], refs[2 * n : 3 * n]
+    sem_in, sem_out = refs[3 * n :]
+    pieces = [(i, part) for i in range(n) for part in range(KEEP[i])]
+
+    def rows(i, part):
+        size = sources[i].shape[0] // KEEP[i]
+        return pl.ds(part * size, size)
+
+    ins = [
+        pltpu.make_async_copy(sources[i].at[rows(i, part)], held[i].at[rows(i, part)], sem_in.at[i, part])
+        for i, part in pieces
+    ]
+    outs = [
+        pltpu.make_async_copy(held[i].at[rows(i, part)], kept[i].at[rows(i, part)], sem_out.at[i, part])
+        for i, part in pieces
+    ]
+    for copy in ins:
+        copy.start()
+    for copy, out in zip(ins, outs):
+        copy.wait()
+        out.start()
+    for out in outs:
+        out.wait()
+
+
+def keep(*arrays):
+    hbm = pl.BlockSpec(memory_space=pltpu.HBM)
+    return pl.pallas_call(
+        keep_kernel,
+        out_shape=tuple(jax.ShapeDtypeStruct(a.shape, a.dtype) for a in arrays),
+        in_specs=[hbm] * len(arrays),
+        out_specs=(hbm,) * len(arrays),
+        scratch_shapes=[pltpu.VMEM(a.shape, a.dtype) for a in arrays]
+        + [pltpu.SemaphoreType.DMA((len(arrays), max(KEEP)))] * 2,
+        compiler_params=pltpu.CompilerParams(vmem_limit_bytes=60 * 1024 * 1024),
+        name="keep",
+    )(*arrays)
+
+
 def body(out_grad, routes, combine, gate_up_weight, down_weight, saved_inputs, saved_gate_up):
     picks = jnp.concatenate([routes[0].T.astype(F32), combine[0].T.astype(F32)], axis=0)
     passed, comb, gu_grad, dn_grad, _, _ = layer(
         out_grad[0], picks, gate_up_weight[0, 0], down_weight[0, 0], saved_inputs[0, 0, 0], saved_gate_up[0, 0, 0]
     )
+    passed, gu_grad, dn_grad = keep(passed, gu_grad, dn_grad)
     return passed[None], comb.T.astype(BF)[None], gu_grad[None, None], dn_grad[None, None]
 
 

time: 127 us -> 122 us (0.961)
  local copies, waits for them, and re-layouts: 8.24 us -> 0.01 us
  Pallas kernels: 114 us -> 118 us
    unnamed x5 -> x2, local copies, waits for them, and re-layouts: 8.24 us -> 0.01 us
    pallas_call x0 -> x1, Pallas kernels: none -> 6.24 us  [keep(): pl.pallas_call(keep_kernel, out_shape=tuple((jax.ShapeDtypeStruct(a.shape...]
    pallas_call x1, Pallas kernels: 114 us -> 112 us  [layer(): pl.pallas_call(layer_kernel, out_shape=(jax.ShapeDtypeStruct((TOK, 2 * wi...]
where the time goes in v4:
time: 122 us
  Pallas kernels  118 us (97%)
  other arithmetic  2.56 us (2%)
    pallas_call x1, Pallas kernels, layer(): pl.pallas_call(layer_kernel, out_shape=(jax.ShapeDtypeStruct((TOK, 2 * wi...  112 us
    pallas_call x1, Pallas kernels, keep(): pl.pallas_call(keep_kernel, out_shape=tuple((jax.ShapeDtypeStruct(a.shape...  6.24 us

profile of v4, /device:TPU:0, one launch (start us, length us, event | category | flops | bytes accessed | tf_op | source)
XLA Modules:
  0.0 121.5 jit_solution(3106534003316497843)
XLA Ops:
  0.6 0.7 fusion
  1.3 0.7 convert_bitcast_fusion
  2.0 0.6 pad_maximum_fusion.picks
  2.6 112.1 %layer.1 = (bf16[128,2560]{1,0:T(8,128)(2,1)}, f32[6,128]{1,0:T(8,128)}, bf16[1280,1792]{1,0:T(8,128)(2,1)}, bf16[896,1280]{1,0:T(8,128)(2,1)}, bf16[1280,1792]{1,0:T(8,128)(2,1)}, /*index=5*/bf16[896,1280]{1,0:T(8,128)(2,1)}) custom-call(bf16[128,2560]{1,0:T(8,128)(2,1)} %bitcast.25, f32[12,128]{1,0:T(8,128)} %pad_maximum_fusion.picks, ...), custom_call_target="tpu_custom_call" | custom-call | tf_op jit(solution)/shard_map/layer/pallas_call | solution.py:479
  114.7 0.0 copy-start
  114.7 6.2 %keep.1 = (bf16[128,2560]{1,0:T(8,128)(2,1)}, bf16[1280,1792]{1,0:T(8,128)(2,1)}, bf16[896,1280]{1,0:T(8,128)(2,1)}) custom-call(bf16[128,2560]{1,0:T(8,128)(2,1)} %get-tuple-element.11.refs_0_, bf16[1280,1792]{1,0:T(8,128)(2,1)} %get-tuple-element.12.refs_1_, bf16[896,1280]{1,0:T(8,128)(2,1)} %get-tuple-element.13.refs_2_), custom_call_target="tpu_custom_call" | custom-call | tf_op jit(solution)/shard_map/keep/pallas_call | solution.py:571
  120.9 0.0 copy-done
  121.0 0.6 convert_bitcast_fusion.1
Async XLA Ops:
  114.7 6.3 %copy-start = (f32[6,128]{1,0:T(8,128)S(1)}, f32[6,128]{1,0:T(8,128)}, u32[]{:S(2)}) copy-start(f32[6,128]{1,0:T(8,128)} %get-tuple-element.15) | copy-start | bytes 9220
